TPU v7x, 32 devices: a whole 2x2x4 slice. The times are simulated.
32 devices in a mesh: shard: 8 (over z, x), tensor: 4 (over y, core).
Axes of the slice: x: 2, y: 2, z: 4, core: 2. Of those that a mesh axis runs over, the one named last changes fastest.
Arguments:
- gradients: bfloat16 [8, 1152, 1152], P(None, 'shard', 'tensor')
- weights: float32 [8, 1152, 1152], P(None, 'shard', 'tensor'), may hold values from -0.1875 to 0.1875
- owner_list: int32 [8], replicated, may hold values from 0 to 7, as said below
- left_gram_stats: float32 [16, 1152, 1152], P('shard', 'tensor'), may hold values from -6 to 6
- right_gram_stats: float32 [16, 1152, 1152], P('shard', 'tensor'), may hold values from -6 to 6
- left_root: bfloat16 [16, 1152, 1152], P('shard', None, 'tensor'), as said below
- right_root: bfloat16 [16, 1152, 1152], P('shard', None, 'tensor'), as said below
- adam_second_moment: float32 [16, 1152, 1152], P('shard', None, 'tensor'), may hold values from 0.1 to 10
Outputs:
- new_weights: float32 [8, 1152, 1152], P(None, 'shard', 'tensor')
- new_left: float32 [16, 1152, 1152], P('shard', 'tensor')
- new_right: float32 [16, 1152, 1152], P('shard', 'tensor')
- new_moment: float32 [16, 1152, 1152], P('shard', None, 'tensor')
Inputs may be any that keep to these rules, and one draw needn't show every extreme that they name: `owner_list`: each owner index is named by at most 2 blocks, and some index by exactly 2. `left_root`: each slot's matrix is symmetric. `right_root`: each slot's matrix is symmetric.
All inputs are finite; a program needn't handle non-finite values.
Results may differ from a plain program's by a relative error of at most 0.0022.
Values may be sent and summed in bfloat16 or wider, within the bound.
A program may use at most 128 MiB of HBM per device.

v0:
```python
import jax
import jax.numpy as jnp
from jax import lax
from jax.sharding import PartitionSpec as P

MODEL_WIDTH = 1152
SLOTS = 2


stat_decay = 0.95
moment_decay = 0.95
learn_rate = 0.02
graft_eps = 1e-06


def slot_table(owner_list):
    count = owner_list.shape[0]
    positions = jnp.arange(count, dtype=jnp.int32)
    earlier = (owner_list[:, None] == owner_list[None, :]) & (
        positions[None, :] < positions[:, None]
    )
    slot_rank = jnp.sum(earlier.astype(jnp.int32), axis=1)
    return (slot_rank, owner_list * SLOTS + slot_rank)


def body(
    gradients,
    weights,
    owner_list,
    left_gram_stats,
    right_gram_stats,
    left_root,
    right_root,
    adam_second_moment,
):
    shard_count = lax.axis_size("shard")
    tensor_count = lax.axis_size("tensor")
    slots = left_gram_stats.shape[0]
    row_count = gradients.shape[1]
    part_width = gradients.shape[2]
    block_count = owner_list.shape[0]
    slot_rank, slot_index = slot_table(owner_list)
    all_slots = jnp.arange(shard_count * slots, dtype=jnp.int32)
    block_ids = jnp.arange(block_count, dtype=jnp.int32)
    matches = slot_index[None, :] == all_slots[:, None]
    occupied = jnp.any(matches, axis=1)
    source_block = jnp.sum(jnp.where(matches, block_ids[None, :], 0), axis=1)
    outgoing = jnp.where(
        occupied[:, None, None],
        jnp.take(gradients, source_block, axis=0),
        jnp.zeros((), jnp.bfloat16),
    )
    layered = outgoing.reshape(shard_count, 1, slots, row_count, part_width)
    layered = jnp.broadcast_to(layered, (shard_count, tensor_count, slots, row_count, part_width))
    layered = layered.reshape(shard_count * tensor_count * slots, row_count, part_width)
    arrived = lax.all_to_all(layered, ("shard", "tensor"), split_axis=0, concat_axis=0, tiled=True)
    arrived = arrived.reshape(shard_count, tensor_count, slots, row_count, part_width)
    full_grad = jnp.transpose(arrived, (2, 0, 3, 1, 4)).reshape(
        slots, shard_count * row_count, tensor_count * part_width
    )
    tensor_pos = lax.axis_index("tensor")
    own_start = tensor_pos * part_width
    grad_rows = lax.dynamic_slice_in_dim(full_grad, own_start, part_width, 1)
    grad_cols = lax.dynamic_slice_in_dim(full_grad, own_start, part_width, 2)
    gram_left = (
        jnp.einsum("sij,skj->sik", grad_rows, full_grad, preferred_element_type=jnp.float32)
        / MODEL_WIDTH
    )
    gram_right = (
        jnp.einsum("sji,sjk->sik", grad_cols, full_grad, preferred_element_type=jnp.float32)
        / MODEL_WIDTH
    )
    new_left = stat_decay * left_gram_stats + gram_left
    new_right = stat_decay * right_gram_stats + gram_right
    grad_part = grad_cols.astype(jnp.float32)
    new_moment = moment_decay * adam_second_moment + (1.0 - moment_decay) * grad_part * grad_part
    adam_dir = grad_part / jnp.sqrt(new_moment)
    product = jnp.einsum(
        "sij,sjk->sik", full_grad, right_root, preferred_element_type=jnp.float32
    ).astype(jnp.bfloat16)
    precond = jnp.einsum(
        "sij,sjk->sik",
        lax.all_gather(left_root, "tensor", axis=2, tiled=True),
        product,
        preferred_element_type=jnp.float32,
    )
    adam_sum = jnp.sum(adam_dir * adam_dir, axis=(1, 2))
    precond_sum = jnp.sum(precond * precond, axis=(1, 2))
    adam_total, precond_total = lax.psum((adam_sum, precond_sum), "tensor")
    entries = float(MODEL_WIDTH * MODEL_WIDTH)
    ratio = jnp.sqrt(adam_total / entries) / jnp.sqrt(precond_total / entries + graft_eps)
    update = (-learn_rate * ratio)[:, None, None] * precond
    update = update.reshape(slots, shard_count, row_count, part_width)
    returned = lax.all_to_all(update, "shard", split_axis=1, concat_axis=1, tiled=True)
    returned = jnp.transpose(returned, (1, 0, 2, 3)).reshape(
        shard_count * slots, row_count, part_width
    )
    block_update = jnp.take(returned, slot_index, axis=0)
    new_weights = weights + block_update
    return (new_weights, new_left, new_right, new_moment)


def solution(mesh):
    return jax.shard_map(
        body,
        mesh=mesh,
        in_specs=(
            P(None, "shard", "tensor"),
            P(None, "shard", "tensor"),
            P(),
            P("shard", "tensor", None),
            P("shard", "tensor", None),
            P("shard", None, "tensor"),
            P("shard", None, "tensor"),
            P("shard", None, "tensor"),
        ),
        out_specs=(
            P(None, "shard", "tensor"),
            P("shard", "tensor", None),
            P("shard", "tensor", None),
            P("shard", None, "tensor"),
        ),
        check_vma=False,
    )
```

profile of v0, /device:TPU:0, one launch (start us, length us, event | category | flops | bytes accessed | tf_op | source)
XLA Modules:
  0.0 331.5 jit_solution(16773509211798116607)
XLA Ops:
  7.2 1.0 convert_reduce_fusion
  8.1 0.7 compare_and_fusion.1
  9.2 2.1 gather_fusion
  11.3 0.3 select_select_fusion
  11.6 3.7 %broadcast_in_dim.70 = bf16[8,4,2,144,288]{4,3,2,1,0:T(8,128)(2,1)} broadcast(bf16[8,2,144,288]{3,2,1,0:T(8,128)(2,1)S(1)} %select_select_fusion), dimensions={0,2,3,4} | broadcast | bytes 6635520 | tf_op jit(solution)/shard_map/broadcast_in_dim | solution.py:54
  15.3 7.4 %all-to-all-start = ((bf16[64,144,288]{2,1,0:T(8,128)(2,1)}), bf16[64,144,288]{2,1,0:T(8,128)(2,1)}, u32[]{:S(2)}, u32[]{:S(2)}) async-start(bf16[64,144,288]{2,1,0:T(8,128)(2,1)} %bitcast.20), calls=%async_computation | async-start | bytes 14155776 | tf_op jit(solution)/shard_map/all_to_all | solution.py:56
  22.7 0.7 all-gather.2.cloned.1.call-update
  23.4 3.7 %copy.28 = f32[2,1152,288]{2,1,0:T(8,128)} copy(f32[2,1152,288]{1,2,0:T(8,128)} %param.15) | data formatting | bytes 5308416 | tf_op args[7]
  27.1 152.5 %all-to-all-done = bf16[64,144,288]{2,1,0:T(8,128)(2,1)} async-done(((bf16[64,144,288]{2,1,0:T(8,128)(2,1)}), bf16[64,144,288]{2,1,0:T(8,128)(2,1)}, u32[]{:S(2)}, u32[]{:S(2)}) %all-to-all-start) | async-done | bytes 5308448 | tf_op jit(solution)/shard_map/all_to_all | solution.py:56
  179.6 9.6 %copy.27 = bf16[2,8,144,4,288]{4,3,2,1,0:T(4,128)(2,1)} copy(bf16[2,8,144,4,288]{4,2,0,3,1:T(8,128)(2,1)} %bitcast.5) | data formatting | bytes 10616832 | tf_op jit(solution)/shard_map/transpose | solution.py:58
  189.2 11.7 %reshape.68 = bf16[2,1152,1152]{2,1,0:T(8,128)(2,1)} reshape(bf16[2,8,144,4,288]{4,3,2,1,0:T(4,128)(2,1)} %copy.27) | data formatting | bytes 10616832 | tf_op jit(solution)/shard_map/reshape | solution.py:58
  200.9 6.2 %fusion.1 = (f32[2]{0:T(128)S(1)}, f32[2,1152,288]{2,1,0:T(8,128)}) fusion(bf16[2,1152,1152]{2,1,0:T(8,128)(2,1)} %reshape.68, s32[]{:T(128)S(6)} %select_n.56, f32[2,1152,288]{2,1,0:T(8,128)} %copy.28), kind=kLoop, calls=%fused_computation.7 | loop fusion | flops 5308414 | bytes 6635532 | tf_op jit(solution)/shard_map/reduce_sum | solution.py:87
  207.1 9.6 %multiply_reduce_fusion = (f32[2]{0:T(128)S(1)}, f32[2,288,1152]{2,1,0:T(8,128)}) fusion(bf16[2,1152,1152]{1,2,0:T(8,128)(2,1)} %all-gather.2.cloned.1.call-done, bf16[2,1152,1152]{2,1,0:T(8,128)(2,1)} %reshape.68, bf16[2,1152,288]{1,2,0:T(8,128)(2,1)S(1)} %copy-done), kind=kOutput, calls=%fused_computation.13 | convolution fusion | flops 3059638272 | bytes 14598152 | tf_op jit(solution)/shard_map/sij,sjk->sik/dot_general | solution.py:81
  216.7 5.7 %all-reduce = (f32[2]{0:T(128)S(1)}, f32[2]{0:T(128)S(1)}) all-reduce(f32[2]{0:T(128)S(1)} %get-tuple-element.26, f32[2]{0:T(128)S(1)} %get-tuple-element.24), channel_id=1, replica_groups=mesh['shard'=8,'tensor'=4] {'tensor'}, use_global_device_ids=true, to_apply=%region_6.7 | all-reduce | flops 4 | bytes 32 | tf_op jit(solution)/shard_map/psum | solution.py:89
  222.4 3.5 %multiply_bitcast_fusion = f32[2,1152,288]{1,2,0:T(8,128)} fusion(f32[2,288,1152]{2,1,0:T(8,128)} %get-tuple-element.27, f32[2]{0:T(128)S(1)} %multiply_multiply_fusion.1), kind=kLoop, calls=%fused_computation.12 | loop fusion | flops 663552 | bytes 5308424 | tf_op jit(solution)/shard_map/mul | solution.py:92
  225.9 3.6 %copy.29 = f32[2,1152,288]{2,1,0:T(8,128)} copy(f32[2,1152,288]{1,2,0:T(8,128)} %multiply_bitcast_fusion) | data formatting | bytes 5308416 | tf_op jit(solution)/shard_map/mul | solution.py:92
  229.6 4.1 %copy.30 = f32[2,8,144,288]{3,2,0,1:T(8,128)} copy(f32[2,8,144,288]{3,2,1,0:T(8,128)} %bitcast.21) | data formatting | bytes 5308416 | tf_op jit(solution)/shard_map/reshape | solution.py:93
  233.6 7.4 %all-to-all-start.1 = ((f32[2,8,144,288]{3,2,0,1:T(8,128)}), f32[2,8,144,288]{3,2,0,1:T(8,128)}, u32[]{:S(2)}, u32[]{:S(2)}) async-start(f32[2,8,144,288]{3,2,0,1:T(8,128)} %copy.30), calls=%async_computation.1 | async-start | bytes 7077888 | tf_op jit(solution)/shard_map/all_to_all | solution.py:94
  241.1 3.7 %copy.32 = f32[2,1152,288]{1,2,0:T(8,128)} copy(f32[2,1152,288]{2,1,0:T(8,128)} %get-tuple-element.25) | data formatting | bytes 5308416
  244.8 8.2 %fusion.3 = f32[2,288,1152]{2,1,0:T(8,128)} fusion(bf16[2,1152,1152]{2,1,0:T(8,128)(2,1)} %reshape.68, f32[2,288,1152]{2,1,0:T(8,128)} %param.12, s32[]{:T(128)S(6)} %select_n.56), kind=kOutput, calls=%fused_computation.9 | convolution fusion | flops 1530814464 | bytes 12386308 | tf_op jit(solution)/shard_map/sji,sjk->sik/dot_general | solution.py:70
  252.9 3.7 %fusion.4 = f32[2,288,1152]{2,1,0:T(8,128)} fusion(bf16[2,1152,1152]{2,1,0:T(8,128)(2,1)S(1)} %bitcast.23, f32[2,288,1152]{2,1,0:T(8,128)S(1)} %copy-done.2, s32[]{:T(128)S(6)} %select_n.56), kind=kOutput, calls=%fused_computation.10 | convolution fusion | flops 1530814464 | bytes 11943940 | tf_op jit(solution)/shard_map/sij,skj->sik/dot_general | solution.py:66
  256.7 62.3 %all-to-all-done.1 = f32[2,8,144,288]{3,2,0,1:T(8,128)} async-done(((f32[2,8,144,288]{3,2,0,1:T(8,128)}), f32[2,8,144,288]{3,2,0,1:T(8,128)}, u32[]{:S(2)}, u32[]{:S(2)}) %all-to-all-start.1) | async-done | bytes 2654240 | tf_op jit(solution)/shard_map/all_to_all | solution.py:94
  319.0 2.7 gather_fusion.1
  321.6 3.0 select_add_fusion
  (23 shorter events, 0.4 us)
Async XLA Ops:
  7.2 200.0 %copy-start = (bf16[2,1152,288]{1,2,0:T(8,128)(2,1)S(1)}, bf16[2,1152,288]{1,2,0:T(8,128)(2,1)}, u32[]{:S(2)}) copy-start(bf16[2,1152,288]{1,2,0:T(8,128)(2,1)} %param.14) | copy-start | bytes 3981316
  15.3 164.4 %all-to-all-start = ((bf16[64,144,288]{2,1,0:T(8,128)(2,1)}), bf16[64,144,288]{2,1,0:T(8,128)(2,1)}, u32[]{:S(2)}, u32[]{:S(2)}) async-start(bf16[64,144,288]{2,1,0:T(8,128)(2,1)} %bitcast.20), calls=%async_computation | async-start | bytes 14155776 | tf_op jit(solution)/shard_map/all_to_all | solution.py:56
  22.7 184.4 %all-gather.2.cloned.1.call-start = ((), (), s32[]{:S(2)}) async-start(), calls=%async_computation.2 | async-start | bytes 6635520 | tf_op jit(solution)/shard_map/all_gather | solution.py:83
  233.6 85.3 %all-to-all-start.1 = ((f32[2,8,144,288]{3,2,0,1:T(8,128)}), f32[2,8,144,288]{3,2,0,1:T(8,128)}, u32[]{:S(2)}, u32[]{:S(2)}) async-start(f32[2,8,144,288]{3,2,0,1:T(8,128)} %copy.30), calls=%async_computation.1 | async-start | bytes 7077888 | tf_op jit(solution)/shard_map/all_to_all | solution.py:94
  241.1 11.9 %slice-start = ((s8[5308416]{0:T(1024)(128)(4,1)}), s8[1114112]{0:T(1024)(128)(4,1)S(1)}, s32[]{:S(2)}) async-start(s8[5308416]{0:T(1024)(128)(4,1)} %bitcast.22), calls=%async_computation.3 | async-start | bytes 2228224
  244.7 8.2 %slice-start.1 = ((s8[5308416]{0:T(1024)(128)(4,1)}), s8[4194304]{0:T(1024)(128)(4,1)S(1)}, s32[]{:S(2)}) async-start(s8[5308416]{0:T(1024)(128)(4,1)} %bitcast.22), calls=%async_computation.4 | async-start | bytes 8388608
  244.7 8.2 %copy-start.2 = (f32[2,288,1152]{2,1,0:T(8,128)S(1)}, f32[2,288,1152]{2,1,0:T(8,128)}, u32[]{:S(2)}) copy-start(f32[2,288,1152]{2,1,0:T(8,128)} %param.11) | copy-start | bytes 7962628
  321.6 3.0 copy-start.1
Sparse Core Ops, SparseCore 0:
  25.1 94.3 all-gather.1
where the time goes:
time: 332 us
  waiting for transfers between devices  216 us (65%)
  local copies, waits for them, and re-layouts  45 us (14%)
  matrix products  21.5 us (6%)
  other arithmetic  14.9 us (4%)
  starting transfers between devices  14.8 us (4%)
  between operations  14.1 us (4%)
  blocking collectives  5.73 us (2%)
    all_to_all x1, waiting for transfers between devices, body(): lax.all_to_all(layered, ('shard', 'tensor'), split_axis=0, concat_axis=0,...  153 us
    all_to_all x1, waiting for transfers between devices, body(): lax.all_to_all(update, 'shard', split_axis=1, concat_axis=1, tiled=True)  62.3 us
    reshape x1, local copies, waits for them, and re-layouts, body(): jnp.transpose(arrived, (2, 0, 3, 1, 4))  11.7 us
    transpose x1, local copies, waits for them, and re-layouts, body(): jnp.transpose(arrived, (2, 0, 3, 1, 4))  9.6 us
    dot_general x1, matrix products, body(): jnp.einsum('sij,sjk->sik', lax.all_gather(left_root, 'tensor', axis=2, ti...  9.57 us
    dot_general x1, matrix products, body(): jnp.einsum('sji,sjk->sik', grad_cols, full_grad, preferred_element_type=j...  8.18 us
    all_to_all x1, starting transfers between devices, body(): lax.all_to_all(layered, ('shard', 'tensor'), split_axis=0, concat_axis=0,...  7.41 us
    unnamed x12, local copies, waits for them, and re-layouts  7.41 us
  transfers between devices with their start and end apart: 3, of which 2 were waited for; matrix products, arithmetic and copies ran while one was open for 14% of the time, Pallas kernels for 0%

commit v1 on v0

--- a/solution.py
+++ b/solution.py
@@ -1,6 +1,10 @@
+import functools
+
 import jax
 import jax.numpy as jnp
 from jax import lax
+from jax.experimental import pallas as pl
+from jax.experimental.pallas import tpu as pltpu
 from jax.sharding import PartitionSpec as P
 
 MODEL_WIDTH = 1152
@@ -100,9 +104,477 @@
     return (new_weights, new_left, new_right, new_moment)
 
 
+MESH = pl.DeviceIdType.MESH
+TILE = 384
+NT = (((1,), (1,)), ((), ()))
+NN = (((1,), (0,)), ((), ()))
+
+
+def mm(a, b, dims):
+    return lax.dot_general(a, b, dims, preferred_element_type=jnp.float32)
+
+
+def step_kernel(
+    shards,
+    owner_ref,
+    grad_ref,
+    right_root_ref,
+    left_root_hbm,
+    left_hbm,
+    right_hbm,
+    moment_hbm,
+    update_ref,
+    new_left_hbm,
+    new_right_hbm,
+    new_moment_hbm,
+    out_buf,
+    own,
+    grad_t,
+    left_root,
+    prod_t,
+    back_out,
+    back_in,
+    left,
+    right,
+    moment,
+    sums,
+    ratios,
+    s1_send,
+    s1_recv,
+    g_send,
+    g_recv,
+    l_send,
+    l_recv,
+    b_send,
+    b_recv,
+    sum_send,
+    sum_recv,
+    rat_send,
+    rat_recv,
+    in_sem,
+    out_sem,
+):
+    me = lax.axis_index("shard")
+    t = lax.axis_index("tensor")
+    sib = t + 1 - 2 * lax.rem(t, 2)
+    across = lax.rem(t + 2, 4)
+    diag = lax.rem(sib + 2, 4)
+    blocks, rows, width = grad_ref.shape
+    side = rows * shards
+    slots = left.shape[0]
+    t_rows = pl.ds(pl.multiple_of(t * width, 32), width)
+    across_rows = pl.ds(pl.multiple_of(across * width, 32), width)
+
+    def peer(d):
+        return lax.rem(me + d, shards)
+
+    def strip(s):
+        return pl.ds(pl.multiple_of(s * rows, 16), rows)
+
+    root_in = [
+        pltpu.make_async_copy(
+            left_root_hbm.at[k], left_root.at[k, t_rows, :], in_sem.at[k]
+        )
+        for k in range(slots)
+    ]
+    stat_in = [
+        pltpu.make_async_copy(src, dst, in_sem.at[slots + i])
+        for i, (src, dst) in enumerate(
+            ((moment_hbm, moment), (left_hbm, left), (right_hbm, right))
+        )
+    ]
+    for copy in root_in:
+        copy.start()
+
+    barrier = pltpu.get_barrier_semaphore()
+
+    @pl.loop(1, shards)
+    def _(d):
+        pl.semaphore_signal(barrier, inc=1, device_id=(peer(d), t), device_id_type=MESH)
+
+    for other in (sib, across, diag):
+        pl.semaphore_signal(barrier, inc=1, device_id=(me, other), device_id_type=MESH)
+
+    owners = [owner_ref[b] for b in range(blocks)]
+    slot_of = []
+    for b in range(blocks):
+        place = owners[b] * slots
+        for c in range(b):
+            place = place + jnp.where(owners[c] == owners[b], 1, 0)
+        slot_of.append(place)
+
+    def pick(k, s):
+        source = jnp.int32(0)
+        found = jnp.int32(0)
+        for b in range(blocks):
+            hit = slot_of[b] == s * slots + k
+            source = jnp.where(hit, b, source)
+            found = jnp.where(hit, 1, found)
+        block = grad_ref[source]
+        return jnp.where(found > 0, block, jnp.zeros_like(block))
+
+    pl.semaphore_wait(barrier, shards - 1 + 3)
+
+    def s1_copy(k, d):
+        s = peer(d)
+        return pltpu.make_async_remote_copy(
+            src_ref=out_buf.at[k, s],
+            dst_ref=own.at[k, strip(me), :],
+            send_sem=s1_send.at[k, s],
+            recv_sem=s1_recv.at[k, me],
+            device_id=(s, t),
+            device_id_type=MESH,
+        )
+
+    def s1_arrival(k, d):
+        s = peer(d)
+        return pltpu.make_async_remote_copy(
+            src_ref=out_buf.at[k, s],
+            dst_ref=own.at[k, strip(s), :],
+            send_sem=s1_send.at[k, s],
+            recv_sem=s1_recv.at[k, s],
+            device_id=(s, t),
+            device_id_type=MESH,
+        )
+
+    def panel_copy(buf, send, recv, k, panel, hop, target):
+        return pltpu.make_async_remote_copy(
+            src_ref=buf.at[k, panel, :],
+            dst_ref=buf.at[k, panel, :],
+            send_sem=send.at[k, hop],
+            recv_sem=recv.at[k, hop],
+            device_id=(me, target),
+            device_id_type=MESH,
+        )
+
+    def root_copies(k):
+        return (
+            panel_copy(left_root, l_send, l_recv, k, t_rows, 0, sib),
+            panel_copy(left_root, l_send, l_recv, k, t_rows, 1, across),
+            panel_copy(left_root, l_send, l_recv, k, across_rows, 2, sib),
+        )
+
+    def grad_copies(k):
+        return (
+            panel_copy(grad_t, g_send, g_recv, k, t_rows, 0, sib),
+            panel_copy(grad_t, g_send, g_recv, k, t_rows, 1, across),
+            panel_copy(grad_t, g_send, g_recv, k, across_rows, 2, sib),
+        )
+
+    def send_strips(k):
+        @pl.loop(1, shards)
+        def _(d):
+            s = peer(d)
+            out_buf[k, s] = pick(k, s)
+            s1_copy(k, d).start()
+
+        own[k, strip(me), :] = pick(k, me)
+
+    root_moves = [root_copies(k) for k in range(slots)]
+    grad_moves = [grad_copies(k) for k in range(slots)]
+
+    send_strips(0)
+    for k in range(slots):
+        root_in[k].wait()
+        root_moves[k][1].start()
+        root_moves[k][0].start()
+        if k + 1 < slots:
+            send_strips(k + 1)
+    for copy in stat_in:
+        copy.start()
+
+    at_row = lax.broadcasted_iota(jnp.int32, (width, width), 0)
+    at_col = lax.broadcasted_iota(jnp.int32, (width, width), 1)
+    unit = (at_row == at_col).astype(jnp.bfloat16)
+
+    def turn_panel(k):
+        @pl.loop(1, shards)
+        def _(d):
+            s1_arrival(k, d).wait_recv()
+
+        for j in range(side // TILE):
+            piece = own[k, j * TILE : (j + 1) * TILE, :]
+            grad_t[k, t_rows, j * TILE : (j + 1) * TILE] = mm(unit, piece, NT).astype(
+                jnp.bfloat16
+            )
+        grad_moves[k][1].start()
+        grad_moves[k][0].start()
+
+    def pass_on(moves):
+        moves[1].wait_recv()
+        moves[2].start()
+
+    chunk = 96
+
+    def moments(k):
+        def one(j, total):
+            at = pl.ds(pl.multiple_of(j * chunk, 32), chunk)
+            g = grad_t[k, pl.ds(pl.multiple_of(t * width + j * chunk, 32), chunk), :].astype(
+                jnp.float32
+            )
+            fresh = moment_decay * moment[k, at, :] + (1.0 - moment_decay) * g * g
+            moment[k, at, :] = fresh
+            direction = g / jnp.sqrt(fresh)
+            return total + jnp.sum(direction * direction, axis=0, keepdims=True)
+
+        total = lax.fori_loop(0, width // chunk, one, jnp.zeros((1, side), jnp.float32))
+        sums[t, 0, k] = jnp.full((8, 128), jnp.sum(total), jnp.float32)
+
+    def back_copy(k, d):
+        s = peer(d)
+        return pltpu.make_async_remote_copy(
+            src_ref=back_out.at[k, s],
+            dst_ref=back_in.at[me * slots + k],
+            send_sem=b_send.at[k, s],
+            recv_sem=b_recv.at[k, me],
+            device_id=(s, t),
+            device_id_type=MESH,
+        )
+
+    def back_arrival(k, d):
+        s = peer(d)
+        return pltpu.make_async_remote_copy(
+            src_ref=back_out.at[k, s],
+            dst_ref=back_in.at[s * slots + k],
+            send_sem=b_send.at[k, s],
+            recv_sem=b_recv.at[k, s],
+            device_id=(s, t),
+            device_id_type=MESH,
+        )
+
+    def precondition(k):
+        @pl.loop(0, side // TILE)
+        def _(j):
+            at = pl.ds(pl.multiple_of(j * TILE, 128), TILE)
+            prod_t[k, :, at] = mm(right_root_ref[k], grad_t[k, :, at], NN).astype(jnp.bfloat16)
+
+        for hop in (0, 2):
+            root_moves[k][hop].wait_recv()
+
+        def piece(s):
+            return mm(left_root[k, strip(s), :], prod_t[k], NT)
+
+        def one(d, total):
+            s = peer(d)
+            part = piece(s)
+            back_out[k, s] = part.astype(jnp.bfloat16)
+            back_copy(k, d).start()
+            return total + jnp.sum(part * part, axis=0, keepdims=True)
+
+        total = lax.fori_loop(1, shards, one, jnp.zeros((1, width), jnp.float32))
+        part = piece(me)
+        back_in[me * slots + k] = part.astype(jnp.bfloat16)
+        total = total + jnp.sum(part * part, axis=0, keepdims=True)
+        sums[t, 1, k] = jnp.full((8, 128), jnp.sum(total), jnp.float32)
+
+    start = pl.multiple_of(t * width // 128 * 128, 128)
+    shift = t * width - start
+    sel_row = lax.broadcasted_iota(jnp.int32, (width, TILE), 0)
+    sel_col = lax.broadcasted_iota(jnp.int32, (width, TILE), 1)
+    select = (sel_col == sel_row + shift).astype(jnp.bfloat16)
+
+    def grams(k):
+        rows_t = mm(select, grad_t[k, :, pl.ds(start, TILE)], NT).astype(jnp.bfloat16)
+        out = []
+
+        @pl.loop(0, side // TILE)
+        def _(j):
+            at = pl.ds(pl.multiple_of(j * TILE, 128), TILE)
+            left[k, :, at] = stat_decay * left[k, :, at] + mm(
+                rows_t, grad_t[k, :, at], NN
+            ) / MODEL_WIDTH
+            right[k, :, at] = stat_decay * right[k, :, at] + mm(
+                grad_t[k, t_rows, :], grad_t[k, at, :], NT
+            ) / MODEL_WIDTH
+
+        for i, (src, dst) in enumerate(
+            ((left, new_left_hbm), (right, new_right_hbm), (moment, new_moment_hbm))
+        ):
+            copy = pltpu.make_async_copy(src.at[k], dst.at[k], out_sem.at[k, i])
+            copy.start()
+            out.append(copy)
+        return out
+
+    for k in range(slots):
+        turn_panel(k)
+        pass_on(root_moves[k])
+    for copy in stat_in:
+        copy.wait()
+    for k in range(slots):
+        moments(k)
+
+    outs = []
+    for k in range(slots):
+        pass_on(grad_moves[k])
+        for hop in (0, 2):
+            grad_moves[k][hop].wait_recv()
+        precondition(k)
+        if k + 1 < slots:
+            outs += grams(k)
+
+    sum_moves = [
+        pltpu.make_async_remote_copy(
+            src_ref=sums.at[t],
+            dst_ref=sums.at[t],
+            send_sem=sum_send.at[i],
+            recv_sem=sum_recv.at[i],
+            device_id=(me, other),
+            device_id_type=MESH,
+        )
+        for i, other in enumerate((sib, across, diag))
+    ]
+    for move in sum_moves:
+        move.start()
+    outs += grams(slots - 1)
+    for move in sum_moves:
+        move.wait_recv()
+
+    entries = float(MODEL_WIDTH * MODEL_WIDTH)
+    totals = sums[0] + sums[1] + sums[2] + sums[3]
+    ratio = jnp.sqrt(totals[0] / entries) / jnp.sqrt(totals[1] / entries + graft_eps)
+    mine = pl.ds(me * slots, slots)
+    ratios[mine] = ratio
+
+    def ratio_copy(d):
+        s = peer(d)
+        return pltpu.make_async_remote_copy(
+            src_ref=ratios.at[mine],
+            dst_ref=ratios.at[mine],
+            send_sem=rat_send.at[s],
+            recv_sem=rat_recv.at[me],
+            device_id=(s, t),
+            device_id_type=MESH,
+        )
+
+    def ratio_arrival(d):
+        s = peer(d)
+        theirs = pl.ds(s * slots, slots)
+        return pltpu.make_async_remote_copy(
+            src_ref=ratios.at[theirs],
+            dst_ref=ratios.at[theirs],
+            send_sem=rat_send.at[s],
+            recv_sem=rat_recv.at[s],
+            device_id=(s, t),
+            device_id_type=MESH,
+        )
+
+    @pl.loop(1, shards)
+    def _(d):
+        ratio_copy(d).start()
+
+    @pl.loop(1, shards)
+    def _(d):
+        ratio_arrival(d).wait_recv()
+        for k in range(slots):
+            back_arrival(k, d).wait_recv()
+
+    for b in range(blocks):
+        scale = -learn_rate * ratios[slot_of[b]][0:1, 0:1]
+        update_ref[b] = scale * back_in[slot_of[b]].astype(jnp.float32)
+
+    @pl.loop(1, shards)
+    def _(d):
+        ratio_copy(d).wait_send()
+        for k in range(slots):
+            s1_copy(k, d).wait_send()
+            back_copy(k, d).wait_send()
+
+    for k in range(slots):
+        for move in root_moves[k] + grad_moves[k]:
+            move.wait_send()
+    for move in sum_moves:
+        move.wait_send()
+    for copy in outs:
+        copy.wait()
+
+
+def kernel_body(
+    gradients,
+    weights,
+    owner_list,
+    left_gram_stats,
+    right_gram_stats,
+    left_root,
+    right_root,
+    adam_second_moment,
+):
+    shards = lax.axis_size("shard")
+    blocks, rows, width = gradients.shape
+    slots = left_gram_stats.shape[0]
+    side = rows * shards
+    bf16, f32 = jnp.bfloat16, jnp.float32
+    flip = lambda a: jnp.transpose(a, (0, 2, 1))
+    hbm = pl.BlockSpec(memory_space=pl.ANY)
+    vmem = pl.BlockSpec(memory_space=pltpu.VMEM)
+    dma = lambda *shape: pltpu.SemaphoreType.DMA(shape)
+    stat = jax.ShapeDtypeStruct((slots, width, side), f32)
+    update, new_left, new_right, new_moment = pl.pallas_call(
+        functools.partial(step_kernel, shards),
+        out_shape=(jax.ShapeDtypeStruct((blocks, rows, width), f32), stat, stat, stat),
+        in_specs=[pl.BlockSpec(memory_space=pltpu.SMEM), vmem, vmem, hbm, hbm, hbm, hbm],
+        out_specs=(vmem, hbm, hbm, hbm),
+        scratch_shapes=[
+            pltpu.VMEM((slots, shards, rows, width), bf16),
+            pltpu.VMEM((slots, side, width), bf16),
+            pltpu.VMEM((slots, side, side), bf16),
+            pltpu.VMEM((slots, side, side), bf16),
+            pltpu.VMEM((slots, width, side), bf16),
+            pltpu.VMEM((slots, shards, rows, width), bf16),
+            pltpu.VMEM((slots * shards, rows, width), bf16),
+            pltpu.VMEM((slots, width, side), f32),
+            pltpu.VMEM((slots, width, side), f32),
+            pltpu.VMEM((slots, width, side), f32),
+            pltpu.VMEM((4, 2, slots, 8, 128), f32),
+            pltpu.VMEM((slots * shards, 8, 128), f32),
+            dma(slots, shards),
+            dma(slots, shards),
+            dma(slots, 3),
+            dma(slots, 3),
+            dma(slots, 3),
+            dma(slots, 3),
+            dma(slots, shards),
+            dma(slots, shards),
+            dma(3),
+            dma(3),
+            dma(shards),
+            dma(shards),
+            dma(slots + 3),
+            dma(slots, 3),
+        ],
+        compiler_params=pltpu.CompilerParams(
+            collective_id=0, has_side_effects=True, vmem_limit_bytes=52 * 2**20
+        ),
+    )(
+        owner_list,
+        gradients,
+        flip(right_root),
+        flip(left_root),
+        left_gram_stats,
+        right_gram_stats,
+        flip(adam_second_moment),
+    )
+    return (weights + update, new_left, new_right, flip(new_moment))
+
+
+def fits(mesh, gradients):
+    shards, tensor = mesh.shape["shard"], mesh.shape["tensor"]
+    rows, width = gradients.shape[1] // shards, gradients.shape[2] // tensor
+    return (
+        tensor == 4
+        and rows % 16 == 0
+        and width % 96 == 0
+        and width <= TILE - 96
+        and gradients.shape[1] % TILE == 0
+    )
+
+
 def solution(mesh):
-    return jax.shard_map(
-        body,
+    def run(gradients, *others):
+        chosen = kernel_body if fits(mesh, gradients) else body
+        return mapped(chosen)(gradients, *others)
+
+    mapped = lambda chosen: jax.shard_map(
+        chosen,
         mesh=mesh,
         in_specs=(
             P(None, "shard", "tensor"),
@@ -122,3 +594,4 @@
         ),
         check_vma=False,
     )
+    return run

time: 332 us -> 113 us (0.34)
  waiting for transfers between devices: 216 us -> 0 us
  Pallas kernels: 0 us -> 99.7 us
  local copies, waits for them, and re-layouts: 45 us -> 8.74 us
  matrix products: 21.5 us -> 0 us
  starting transfers between devices: 14.8 us -> 0 us
  between operations: 14.1 us -> 0.67 us
  other arithmetic: 14.9 us -> 3.05 us
  blocking collectives: 5.73 us -> 0 us
    all_to_all x2 -> x0, waiting for transfers between devices: 215 us -> none  [the longest x1 153 us: body(): lax.all_to_all(layered, ('shard', 'tensor'), split_axis=0, concat_axis=0,...]
    pallas_call x0 -> x1, Pallas kernels: none -> 99.7 us  [kernel_body(): pl.pallas_call(functools.partial(step_kernel, shards), out_shape=(jax.Sha...]
    dot_general x3 -> x0, matrix products: 21.5 us -> none  [the longest x1 9.57 us: body(): jnp.einsum('sij,sjk->sik', lax.all_gather(left_root, 'tensor', axis=2, ti...]
    reshape x2 -> x0, local copies, waits for them, and re-layouts: 15.8 us -> none  [the longest x1 11.7 us: body(): jnp.transpose(arrived, (2, 0, 3, 1, 4))]
    all_to_all x2 -> x0, starting transfers between devices: 14.8 us -> none  [the longest x1 7.41 us: body(): lax.all_to_all(layered, ('shard', 'tensor'), split_axis=0, concat_axis=0,...]
    transpose x1 -> x0, local copies, waits for them, and re-layouts: 9.6 us -> none  [body(): jnp.transpose(arrived, (2, 0, 3, 1, 4))]
    reduce_sum x3 -> x0, other arithmetic: 7.23 us -> none  [the longest x1 6.19 us: body(): adam_sum = jnp.sum(adam_dir * adam_dir, axis=(1, 2))]
    psum x1 -> x0, blocking collectives: 5.73 us -> none  [body(): adam_total, precond_total = lax.psum((adam_sum, precond_sum), 'tensor')]
  transfers between devices with their start and end apart: 3 -> 0, of which waited for: 2 -> 0; matrix products, arithmetic and copies ran while one was open for 14% -> 0% of each run, Pallas kernels for 0% -> 0%
where the time goes in v1:
time: 113 us; the launch traced here: 112 us
  Pallas kernels  99.7 us (88%)
  local copies, waits for them, and re-layouts  8.74 us (8%)
  other arithmetic  3.05 us (3%)
    pallas_call x1, Pallas kernels, kernel_body(): pl.pallas_call(functools.partial(step_kernel, shards), out_shape=(jax.Sha...  99.7 us
    unnamed x15, local copies, waits for them, and re-layouts  8.74 us
    add x1, other arithmetic, kernel_body(): return (weights + update, new_left, new_right, flip(new_moment))  3.05 us

profile of v1, /device:TPU:0, one launch (start us, length us, event | category | flops | bytes accessed | tf_op | source)
XLA Modules:
  0.0 112.2 jit_solution(3737827872685374873)
XLA Ops:
  0.6 0.0 copy-start
  0.6 1.2 %copy-done = bf16[8,144,288]{2,1,0:T(8,128)(2,1)S(1)} copy-done((bf16[8,144,288]{2,1,0:T(8,128)(2,1)S(1)}, bf16[8,144,288]{2,1,0:T(8,128)(2,1)}, u32[]{:S(2)}) %copy-start) | copy-done | bytes 663576
  1.8 0.0 copy-start.1
  1.8 0.7 copy-done.1
  2.5 0.0 copy-start.5
  2.5 99.7 %shard_map.111 = (f32[8,144,288]{2,1,0:T(8,128)}, f32[2,288,1152]{2,1,0:T(8,128)}, f32[2,288,1152]{2,1,0:T(8,128)}, f32[2,288,1152]{2,1,0:T(8,128)}) custom-call(s32[8]{0:T(128)S(1)} %copy-done.1, bf16[8,144,288]{2,1,0:T(8,128)(2,1)S(1)} %copy-done, bf16[2,288,1152]{2,1,0:T(8,128)(2,1)} %bitcast.6, bf16[2,288,1152]{2,1,0:T(8,128)(2,1)} %bitcast.7, ...), custom_call_target="tpu_custom_call" | custom-call | tf_op jit(solution)/shard_map/pallas_call | solution.py:511
  102.2 0.0 copy-done.5
  102.2 0.0 copy-start.4
  102.2 3.1 %add.3 = f32[8,144,288]{2,1,0:T(8,128)} add(f32[8,144,288]{2,1,0:T(8,128)S(1)} %copy-done.5, f32[8,144,288]{2,1,0:T(8,128)} %get-tuple-element.8) | non-fusion elementwise | flops 331776 | bytes 3981312 | tf_op jit(solution)/shard_map/add | solution.py:556
  105.3 0.0 copy-done.4
  105.3 0.0 copy-start.3
  105.3 1.5 %copy.15 = f32[2,288,1152]{2,1,0:T(8,128)} copy(f32[2,288,1152]{2,1,0:T(8,128)S(1)} %copy-done.4) | data formatting | bytes 5308416
  106.8 1.2 %copy-done.3 = f32[2,288,1152]{2,1,0:T(8,128)S(1)} copy-done((f32[2,288,1152]{2,1,0:T(8,128)S(1)}, f32[2,288,1152]{2,1,0:T(8,128)}, u32[]{:S(2)}) %copy-start.3) | copy-done | bytes 2654232
  108.0 0.0 copy-start.2
  108.0 1.5 %copy.16 = f32[2,288,1152]{2,1,0:T(8,128)} copy(f32[2,288,1152]{2,1,0:T(8,128)S(1)} %copy-done.3) | data formatting | bytes 5308416
  109.5 1.2 %copy-done.2 = f32[2,288,1152]{2,1,0:T(8,128)S(1)} copy-done((f32[2,288,1152]{2,1,0:T(8,128)S(1)}, f32[2,288,1152]{2,1,0:T(8,128)}, u32[]{:S(2)}) %copy-start.2) | copy-done | bytes 2654232
  110.7 1.5 %copy.17 = f32[2,1152,288]{1,2,0:T(8,128)} copy(f32[2,1152,288]{1,2,0:T(8,128)S(1)} %bitcast.4) | data formatting | bytes 5308416
Async XLA Ops:
  0.6 1.2 %copy-start = (bf16[8,144,288]{2,1,0:T(8,128)(2,1)S(1)}, bf16[8,144,288]{2,1,0:T(8,128)(2,1)}, u32[]{:S(2)}) copy-start(bf16[8,144,288]{2,1,0:T(8,128)(2,1)} %grad_ref.1) | copy-start | bytes 1990660
  1.8 0.7 copy-start.1
  2.5 99.8 %copy-start.5 = (f32[8,144,288]{2,1,0:T(8,128)S(1)}, f32[8,144,288]{2,1,0:T(8,128)}, u32[]{:S(2)}) copy-start(f32[8,144,288]{2,1,0:T(8,128)} %param.9) | copy-start | bytes 3981316
  102.2 3.1 %copy-start.4 = (f32[2,288,1152]{2,1,0:T(8,128)S(1)}, f32[2,288,1152]{2,1,0:T(8,128)}, u32[]{:S(2)}) copy-start(f32[2,288,1152]{2,1,0:T(8,128)} %get-tuple-element.17) | copy-start | bytes 7962628
  105.3 2.7 %copy-start.3 = (f32[2,288,1152]{2,1,0:T(8,128)S(1)}, f32[2,288,1152]{2,1,0:T(8,128)}, u32[]{:S(2)}) copy-start(f32[2,288,1152]{2,1,0:T(8,128)} %get-tuple-element.18) | copy-start | bytes 7962628
  108.0 2.7 %copy-start.2 = (f32[2,288,1152]{2,1,0:T(8,128)S(1)}, f32[2,288,1152]{2,1,0:T(8,128)}, u32[]{:S(2)}) copy-start(f32[2,288,1152]{2,1,0:T(8,128)} %get-tuple-element.11) | copy-start | bytes 7962628

commit v2 on v1

--- a/solution.py
+++ b/solution.py
@@ -127,13 +127,18 @@
     new_left_hbm,
     new_right_hbm,
     new_moment_hbm,
-    out_buf,
-    own,
+    out_0,
+    out_1,
+    own_0,
+    own_1,
     grad_t,
     left_root,
     prod_t,
-    back_out,
-    back_in,
+    tail_t,
+    back_0,
+    back_1,
+    in_0,
+    in_1,
     left,
     right,
     moment,
@@ -162,6 +167,14 @@
     blocks, rows, width = grad_ref.shape
     side = rows * shards
     slots = left.shape[0]
+    main = width // 128 * 128
+    tail = width - main
+    wide = main + 128
+    half = 2 * width
+    low, high = half // 128 * 128, -(-half // 128) * 128
+    y = t // 2
+    out_bufs, owns = (out_0, out_1), (own_0, own_1)
+    backs, ins = (back_0, back_1), (in_0, in_1)
     t_rows = pl.ds(pl.multiple_of(t * width, 32), width)
     across_rows = pl.ds(pl.multiple_of(across * width, 32), width)
 
@@ -213,13 +226,25 @@
         block = grad_ref[source]
         return jnp.where(found > 0, block, jnp.zeros_like(block))
 
+    def shifted(count, lanes, shift):
+        row = lax.broadcasted_iota(jnp.int32, (count, lanes), 0)
+        col = lax.broadcasted_iota(jnp.int32, (count, lanes), 1)
+        return (col == row + shift).astype(jnp.bfloat16)
+
+    def pack(s):
+        first, second = pick(0, s), pick(1, s)
+        ends = mm(first[:, main:], shifted(tail, 128, 0), NN) + mm(
+            second[:, main:], shifted(tail, 128, tail), NN
+        )
+        return first[:, :main], ends.astype(jnp.bfloat16), second[:, :main]
+
     pl.semaphore_wait(barrier, shards - 1 + 3)
 
     def s1_copy(k, d):
         s = peer(d)
         return pltpu.make_async_remote_copy(
-            src_ref=out_buf.at[k, s],
-            dst_ref=own.at[k, strip(me), :],
+            src_ref=out_bufs[k].at[s],
+            dst_ref=owns[k].at[strip(me), :],
             send_sem=s1_send.at[k, s],
             recv_sem=s1_recv.at[k, me],
             device_id=(s, t),
@@ -229,29 +254,43 @@
     def s1_arrival(k, d):
         s = peer(d)
         return pltpu.make_async_remote_copy(
-            src_ref=out_buf.at[k, s],
-            dst_ref=own.at[k, strip(s), :],
+            src_ref=out_bufs[k].at[s],
+            dst_ref=owns[k].at[strip(s), :],
             send_sem=s1_send.at[k, s],
             recv_sem=s1_recv.at[k, s],
             device_id=(s, t),
             device_id_type=MESH,
         )
 
-    def panel_copy(buf, send, recv, k, panel, hop, target):
+    def panel_copy(buf, send, recv, k, panel, hop, target, lanes=slice(None)):
         return pltpu.make_async_remote_copy(
-            src_ref=buf.at[k, panel, :],
-            dst_ref=buf.at[k, panel, :],
+            src_ref=buf.at[k, panel, lanes],
+            dst_ref=buf.at[k, panel, lanes],
             send_sem=send.at[k, hop],
             recv_sem=recv.at[k, hop],
             device_id=(me, target),
             device_id_type=MESH,
         )
 
+    def window(which):
+        return pl.ds(pl.multiple_of(low * which, 128), high)
+
+    def mirror(k):
+        root_moves[k][0].wait_recv()
+        turn = shifted(half, high, (half - low) * (1 - y))
+
+        @pl.loop(0, low // 256)
+        def _(j):
+            here = pl.ds(pl.multiple_of(high * y + 256 * j, 128), 256)
+            there = pl.ds(pl.multiple_of(half * (1 - y), 32), half)
+            piece = left_root[k, here, window(1 - y)]
+            left_root[k, there, here] = mm(turn, piece, NT).astype(jnp.bfloat16)
+
     def root_copies(k):
         return (
             panel_copy(left_root, l_send, l_recv, k, t_rows, 0, sib),
-            panel_copy(left_root, l_send, l_recv, k, t_rows, 1, across),
-            panel_copy(left_root, l_send, l_recv, k, across_rows, 2, sib),
+            panel_copy(left_root, l_send, l_recv, k, t_rows, 1, across, window(y)),
+            panel_copy(left_root, l_send, l_recv, k, across_rows, 2, sib, window(1 - y)),
         )
 
     def grad_copies(k):
@@ -261,31 +300,35 @@
             panel_copy(grad_t, g_send, g_recv, k, across_rows, 2, sib),
         )
 
-    def send_strips(k):
-        @pl.loop(1, shards)
-        def _(d):
-            s = peer(d)
-            out_buf[k, s] = pick(k, s)
-            s1_copy(k, d).start()
-
-        own[k, strip(me), :] = pick(k, me)
-
     root_moves = [root_copies(k) for k in range(slots)]
     grad_moves = [grad_copies(k) for k in range(slots)]
 
-    send_strips(0)
+    @pl.loop(1, shards)
+    def _(d):
+        s = peer(d)
+        first, ends, second = pack(s)
+        out_0[s, :, 0:main] = first
+        out_0[s, :, main:wide] = ends
+        out_1[s] = second
+        s1_copy(0, d).start()
+
     for k in range(slots):
         root_in[k].wait()
         root_moves[k][1].start()
         root_moves[k][0].start()
-        if k + 1 < slots:
-            send_strips(k + 1)
+
+    @pl.loop(1, shards)
+    def _(d):
+        s1_copy(1, d).start()
+
+    first, ends, second = pack(me)
+    own_0[strip(me), 0:main] = first
+    own_0[strip(me), main:wide] = ends
+    own_1[strip(me), :] = second
+    prod_t[1, width:, :] = jnp.zeros((wide - width, side), jnp.bfloat16)
+    tail_t[...] = jnp.zeros((128, side), jnp.bfloat16)
     for copy in stat_in:
         copy.start()
-
-    at_row = lax.broadcasted_iota(jnp.int32, (width, width), 0)
-    at_col = lax.broadcasted_iota(jnp.int32, (width, width), 1)
-    unit = (at_row == at_col).astype(jnp.bfloat16)
 
     def turn_panel(k):
         @pl.loop(1, shards)
@@ -293,10 +336,20 @@
             s1_arrival(k, d).wait_recv()
 
         for j in range(side // TILE):
-            piece = own[k, j * TILE : (j + 1) * TILE, :]
-            grad_t[k, t_rows, j * TILE : (j + 1) * TILE] = mm(unit, piece, NT).astype(
-                jnp.bfloat16
-            )
+            at = slice(j * TILE, (j + 1) * TILE)
+            if k == 0:
+                grad_t[0, t_rows, at] = mm(shifted(width, wide, 0), own_0[at, :], NT).astype(
+                    jnp.bfloat16
+                )
+            else:
+                top = pl.ds(pl.multiple_of(t * width, 32), main)
+                end = pl.ds(pl.multiple_of(t * width + main, 32), tail)
+                grad_t[1, top, at] = mm(shifted(main, main, 0), own_1[at, :], NT).astype(
+                    jnp.bfloat16
+                )
+                grad_t[1, end, at] = mm(
+                    shifted(tail, 128, tail), own_0[at, main:wide], NT
+                ).astype(jnp.bfloat16)
         grad_moves[k][1].start()
         grad_moves[k][0].start()
 
@@ -323,8 +376,8 @@
     def back_copy(k, d):
         s = peer(d)
         return pltpu.make_async_remote_copy(
-            src_ref=back_out.at[k, s],
-            dst_ref=back_in.at[me * slots + k],
+            src_ref=backs[k].at[s],
+            dst_ref=ins[k].at[me],
             send_sem=b_send.at[k, s],
             recv_sem=b_recv.at[k, me],
             device_id=(s, t),
@@ -334,8 +387,8 @@
     def back_arrival(k, d):
         s = peer(d)
         return pltpu.make_async_remote_copy(
-            src_ref=back_out.at[k, s],
-            dst_ref=back_in.at[s * slots + k],
+            src_ref=backs[k].at[s],
+            dst_ref=ins[k].at[s],
             send_sem=b_send.at[k, s],
             recv_sem=b_recv.at[k, s],
             device_id=(s, t),
@@ -346,32 +399,54 @@
         @pl.loop(0, side // TILE)
         def _(j):
             at = pl.ds(pl.multiple_of(j * TILE, 128), TILE)
-            prod_t[k, :, at] = mm(right_root_ref[k], grad_t[k, :, at], NN).astype(jnp.bfloat16)
-
-        for hop in (0, 2):
-            root_moves[k][hop].wait_recv()
-
-        def piece(s):
-            return mm(left_root[k, strip(s), :], prod_t[k], NT)
+            prod_t[k, 0:width, at] = mm(right_root_ref[k], grad_t[k, :, at], NN).astype(
+                jnp.bfloat16
+            )
+
+        if k == 0:
+            tail_t[tail : 2 * tail, :] = prod_t[0, main:width, :]
+        root_moves[k][2].wait_recv()
+
+        def squares(part):
+            return jnp.sum(part * part, axis=0, keepdims=True)
+
+        def pieces(s, put, total):
+            if k == 0:
+                part = mm(left_root[0, strip(s), :], prod_t[0, 0:main, :], NT)
+                put(part)
+                return total[0] + squares(part), total[1]
+            part = mm(left_root[1, strip(s), :], prod_t[1], NT)
+            ends = mm(left_root[0, strip(s), :], tail_t[...], NT)
+            put(part, ends)
+            return total[0] + squares(part), total[1] + squares(ends)
+
+        def put_in(ref, s):
+            def put(part, ends=None):
+                if ends is None:
+                    ref[s] = part.astype(jnp.bfloat16)
+                else:
+                    ref[s, :, 0:main] = part[:, 0:main].astype(jnp.bfloat16)
+                    ref[s, :, main:wide] = (part[:, main:wide] + ends).astype(jnp.bfloat16)
+
+            return put
 
         def one(d, total):
             s = peer(d)
-            part = piece(s)
-            back_out[k, s] = part.astype(jnp.bfloat16)
+            total = pieces(s, put_in(backs[k], s), total)
             back_copy(k, d).start()
-            return total + jnp.sum(part * part, axis=0, keepdims=True)
-
-        total = lax.fori_loop(1, shards, one, jnp.zeros((1, width), jnp.float32))
-        part = piece(me)
-        back_in[me * slots + k] = part.astype(jnp.bfloat16)
-        total = total + jnp.sum(part * part, axis=0, keepdims=True)
-        sums[t, 1, k] = jnp.full((8, 128), jnp.sum(total), jnp.float32)
+            return total
+
+        lanes = main if k == 0 else wide
+        none = (jnp.zeros((1, lanes), jnp.float32), jnp.zeros((1, 128), jnp.float32))
+        total = lax.fori_loop(1, shards, one, none)
+        total = pieces(me, put_in(ins[k], me), total)
+        sums[t, 1, k] = jnp.full((8, 128), jnp.sum(total[0]), jnp.float32)
+        if k == 1:
+            sums[t, 1, 0] = sums[t, 1, 0] + jnp.full((8, 128), jnp.sum(total[1]), jnp.float32)
 
     start = pl.multiple_of(t * width // 128 * 128, 128)
     shift = t * width - start
-    sel_row = lax.broadcasted_iota(jnp.int32, (width, TILE), 0)
-    sel_col = lax.broadcasted_iota(jnp.int32, (width, TILE), 1)
-    select = (sel_col == sel_row + shift).astype(jnp.bfloat16)
+    select = shifted(width, TILE, shift)
 
     def grams(k):
         rows_t = mm(select, grad_t[k, :, pl.ds(start, TILE)], NT).astype(jnp.bfloat16)
@@ -396,12 +471,14 @@
         return out
 
     for k in range(slots):
-        turn_panel(k)
+        mirror(k)
+    turn_panel(0)
+    for k in range(slots):
         pass_on(root_moves[k])
     for copy in stat_in:
         copy.wait()
-    for k in range(slots):
-        moments(k)
+    moments(0)
+    turn_panel(1)
 
     outs = []
     for k in range(slots):
@@ -410,6 +487,7 @@
             grad_moves[k][hop].wait_recv()
         precondition(k)
         if k + 1 < slots:
+            moments(k + 1)
             outs += grams(k)
 
     sum_moves = [
@@ -470,7 +548,15 @@
 
     for b in range(blocks):
         scale = -learn_rate * ratios[slot_of[b]][0:1, 0:1]
-        update_ref[b] = scale * back_in[slot_of[b]].astype(jnp.float32)
+        first, second = in_0[owners[b]], in_1[owners[b]]
+        at_first = slot_of[b] == owners[b] * slots
+        ends = second[:, main:wide].astype(jnp.float32)
+        update_ref[b, :, 0:main] = scale * jnp.where(at_first, first, second[:, 0:main]).astype(
+            jnp.float32
+        )
+        update_ref[b, :, main:width] = scale * jnp.where(
+            at_first, ends[:, tail : 2 * tail], ends[:, 0:tail]
+        )
 
     @pl.loop(1, shards)
     def _(d):
@@ -486,6 +572,13 @@
         move.wait_send()
     for copy in outs:
         copy.wait()
+
+
+def finish_kernel(weights, update, left, right, moment, weights_out, left_out, right_out, moment_out):
+    weights_out[...] = weights[...] + update[...]
+    left_out[...] = left[...]
+    right_out[...] = right[...]
+    moment_out[...] = moment[...]
 
 
 def kernel_body(
@@ -502,6 +595,8 @@
     blocks, rows, width = gradients.shape
     slots = left_gram_stats.shape[0]
     side = rows * shards
+    main = width // 128 * 128
+    wide = main + 128
     bf16, f32 = jnp.bfloat16, jnp.float32
     flip = lambda a: jnp.transpose(a, (0, 2, 1))
     hbm = pl.BlockSpec(memory_space=pl.ANY)
@@ -514,13 +609,18 @@
         in_specs=[pl.BlockSpec(memory_space=pltpu.SMEM), vmem, vmem, hbm, hbm, hbm, hbm],
         out_specs=(vmem, hbm, hbm, hbm),
         scratch_shapes=[
-            pltpu.VMEM((slots, shards, rows, width), bf16),
-            pltpu.VMEM((slots, side, width), bf16),
+            pltpu.VMEM((shards, rows, wide), bf16),
+            pltpu.VMEM((shards, rows, main), bf16),
+            pltpu.VMEM((side, wide), bf16),
+            pltpu.VMEM((side, main), bf16),
             pltpu.VMEM((slots, side, side), bf16),
             pltpu.VMEM((slots, side, side), bf16),
-            pltpu.VMEM((slots, width, side), bf16),
-            pltpu.VMEM((slots, shards, rows, width), bf16),
-            pltpu.VMEM((slots * shards, rows, width), bf16),
+            pltpu.VMEM((slots, wide, side), bf16),
+            pltpu.VMEM((128, side), bf16),
+            pltpu.VMEM((shards, rows, main), bf16),
+            pltpu.VMEM((shards, rows, wide), bf16),
+            pltpu.VMEM((shards, rows, main), bf16),
+            pltpu.VMEM((shards, rows, wide), bf16),
             pltpu.VMEM((slots, width, side), f32),
             pltpu.VMEM((slots, width, side), f32),
             pltpu.VMEM((slots, width, side), f32),
@@ -553,24 +653,43 @@
         right_gram_stats,
         flip(adam_second_moment),
     )
-    return (weights + update, new_left, new_right, flip(new_moment))
-
-
-def fits(mesh, gradients):
+    part = slots * width // blocks
+    strip = pl.BlockSpec((1, rows, width), lambda i: (i, 0, 0))
+    band = pl.BlockSpec((1, part, side), lambda i: (i * part // width, i % (width // part), 0))
+    new_weights, new_left, new_right, new_moment = pl.pallas_call(
+        finish_kernel,
+        grid=(blocks,),
+        out_shape=(jax.ShapeDtypeStruct((blocks, rows, width), f32), stat, stat, stat),
+        in_specs=[strip, strip, band, band, band],
+        out_specs=(strip, band, band, band),
+        compiler_params=pltpu.CompilerParams(vmem_limit_bytes=56 * 2**20),
+    )(weights, update, new_left, new_right, new_moment)
+    return (new_weights, new_left, new_right, flip(new_moment))
+
+
+def fits(mesh, gradients, slot_total):
     shards, tensor = mesh.shape["shard"], mesh.shape["tensor"]
-    rows, width = gradients.shape[1] // shards, gradients.shape[2] // tensor
+    blocks, side, _ = gradients.shape
+    rows, width = side // shards, side // tensor
+    slots = slot_total // shards
+    part = slots * width // blocks
     return (
         tensor == 4
+        and slots == 2
         and rows % 16 == 0
         and width % 96 == 0
         and width <= TILE - 96
-        and gradients.shape[1] % TILE == 0
+        and 0 < width % 128 <= 64
+        and side % TILE == 0
+        and (side // 2) // 128 * 128 % 256 == 0
+        and part % 8 == 0
+        and width % part == 0
     )
 
 
 def solution(mesh):
     def run(gradients, *others):
-        chosen = kernel_body if fits(mesh, gradients) else body
+        chosen = kernel_body if fits(mesh, gradients, others[2].shape[0]) else body
         return mapped(chosen)(gradients, *others)
 
     mapped = lambda chosen: jax.shard_map(

time: 113 us -> 102 us (0.903)
  the two profiles are of different devices: /device:TPU:0 before, /device:TPU:25 now
where the time goes in v2:
time: 102 us; the launch traced here: 101 us
  Pallas kernels  98.7 us (97%)
  local copies, waits for them, and re-layouts  1.82 us (2%)
    pallas_call x1, Pallas kernels, kernel_body(): pl.pallas_call(functools.partial(step_kernel, shards), out_shape=(jax.Sha...  88.7 us
    pallas_call x1, Pallas kernels, kernel_body(): pl.pallas_call(finish_kernel, grid=(blocks,), out_shape=(jax.ShapeDtypeSt...  10 us

profile of v2, /device:TPU:25, one launch (start us, length us, event | category | flops | bytes accessed | tf_op | source)
XLA Modules:
  0.0 101.1 jit_solution(17831496906381042614)
XLA Ops:
  0.6 0.0 copy-start
  0.6 1.2 %copy-done = bf16[8,144,288]{2,1,0:T(8,128)(2,1)S(1)} copy-done((bf16[8,144,288]{2,1,0:T(8,128)(2,1)S(1)}, bf16[8,144,288]{2,1,0:T(8,128)(2,1)}, u32[]{:S(2)}) %copy-start) | copy-done | bytes 663576
  1.8 0.0 copy-start.1
  1.8 0.7 copy-done.1
  2.5 88.7 %shard_map.111 = (f32[8,144,288]{2,1,0:T(8,128)}, f32[2,288,1152]{2,1,0:T(8,128)}, f32[2,288,1152]{2,1,0:T(8,128)}, f32[2,288,1152]{2,1,0:T(8,128)}) custom-call(s32[8]{0:T(128)S(1)} %copy-done.1, bf16[8,144,288]{2,1,0:T(8,128)(2,1)S(1)} %copy-done, bf16[2,288,1152]{2,1,0:T(8,128)(2,1)} %bitcast.5, bf16[2,288,1152]{2,1,0:T(8,128)(2,1)} %bitcast.6, ...), custom_call_target="tpu_custom_call" | custom-call | tf_op jit(solution)/shard_map/pallas_call | solution.py:606
  91.1 10.0 %shard_map.112 = (f32[8,144,288]{2,1,0:T(8,128)}, f32[2,288,1152]{2,1,0:T(8,128)}, f32[2,288,1152]{2,1,0:T(8,128)}, f32[2,288,1152]{2,1,0:T(8,128)}) custom-call(f32[8,144,288]{2,1,0:T(8,128)} %weights.1, f32[8,144,288]{2,1,0:T(8,128)} %get-tuple-element.12.update, f32[2,288,1152]{2,1,0:T(8,128)} %get-tuple-element.13.left, ...), custom_call_target="tpu_custom_call" | custom-call | tf_op jit(solution)/shard_map/pallas_call | solution.py:659
Async XLA Ops:
  0.6 1.2 %copy-start = (bf16[8,144,288]{2,1,0:T(8,128)(2,1)S(1)}, bf16[8,144,288]{2,1,0:T(8,128)(2,1)}, u32[]{:S(2)}) copy-start(bf16[8,144,288]{2,1,0:T(8,128)(2,1)} %grad_ref.1) | copy-start | bytes 1990660
  1.8 0.7 copy-start.1

commit v3 on v2

--- a/solution.py
+++ b/solution.py
@@ -106,6 +106,8 @@
 
 MESH = pl.DeviceIdType.MESH
 TILE = 384
+PIECES = 3
+EARLY = 5
 NT = (((1,), (1,)), ((), ()))
 NN = (((1,), (0,)), ((), ()))
 
@@ -176,7 +178,11 @@
     out_bufs, owns = (out_0, out_1), (own_0, own_1)
     backs, ins = (back_0, back_1), (in_0, in_1)
     t_rows = pl.ds(pl.multiple_of(t * width, 32), width)
-    across_rows = pl.ds(pl.multiple_of(across * width, 32), width)
+    cut = width // PIECES
+
+    def panel(device, c):
+        return pl.ds(pl.multiple_of(device * width + c * cut, 32), cut)
+
 
     def peer(d):
         return lax.rem(me + d, shards)
@@ -286,25 +292,47 @@
             piece = left_root[k, here, window(1 - y)]
             left_root[k, there, here] = mm(turn, piece, NT).astype(jnp.bfloat16)
 
+    def root_across(k, c):
+        return panel_copy(
+            left_root, l_send, l_recv, k, panel(t, c), 1 + c, across, window(y)
+        )
+
     def root_copies(k):
         return (
             panel_copy(left_root, l_send, l_recv, k, t_rows, 0, sib),
-            panel_copy(left_root, l_send, l_recv, k, t_rows, 1, across, window(y)),
-            panel_copy(left_root, l_send, l_recv, k, across_rows, 2, sib, window(1 - y)),
+            [root_across(k, c) for c in range(PIECES)],
+            [
+                panel_copy(
+                    left_root,
+                    l_send,
+                    l_recv,
+                    k,
+                    panel(across, c),
+                    1 + PIECES + c,
+                    sib,
+                    window(1 - y),
+                )
+                for c in range(PIECES)
+            ],
         )
 
     def grad_copies(k):
         return (
             panel_copy(grad_t, g_send, g_recv, k, t_rows, 0, sib),
-            panel_copy(grad_t, g_send, g_recv, k, t_rows, 1, across),
-            panel_copy(grad_t, g_send, g_recv, k, across_rows, 2, sib),
+            [
+                panel_copy(grad_t, g_send, g_recv, k, panel(t, c), 1 + c, across)
+                for c in range(PIECES)
+            ],
+            [
+                panel_copy(grad_t, g_send, g_recv, k, panel(across, c), 1 + PIECES + c, sib)
+                for c in range(PIECES)
+            ],
         )
 
     root_moves = [root_copies(k) for k in range(slots)]
     grad_moves = [grad_copies(k) for k in range(slots)]
 
-    @pl.loop(1, shards)
-    def _(d):
+    def send_first(d):
         s = peer(d)
         first, ends, second = pack(s)
         out_0[s, :, 0:main] = first
@@ -312,12 +340,20 @@
         out_1[s] = second
         s1_copy(0, d).start()
 
+    for copy in root_in:
+        copy.wait()
+
+    @pl.loop(0, slots * PIECES)
+    def _(i):
+        send_first(i + 1)
+        root_across(i // PIECES, lax.rem(i, PIECES)).start()
+
+    for d in range(slots * PIECES + 1, shards):
+        send_first(d)
     for k in range(slots):
-        root_in[k].wait()
-        root_moves[k][1].start()
         root_moves[k][0].start()
 
-    @pl.loop(1, shards)
+    @pl.loop(1, EARLY)
     def _(d):
         s1_copy(1, d).start()
 
@@ -350,12 +386,20 @@
                 grad_t[1, end, at] = mm(
                     shifted(tail, 128, tail), own_0[at, main:wide], NT
                 ).astype(jnp.bfloat16)
-        grad_moves[k][1].start()
+        for c in range(PIECES):
+            grad_moves[k][1][c].start()
+            if k == 0 and EARLY + c < shards:
+                s1_copy(1, EARLY + c).start()
         grad_moves[k][0].start()
 
     def pass_on(moves):
-        moves[1].wait_recv()
-        moves[2].start()
+        for c in range(PIECES):
+            moves[1][c].wait_recv()
+            moves[2][c].start()
+
+    def arrived(moves):
+        for c in range(PIECES):
+            moves[2][c].wait_recv()
 
     chunk = 96
 
@@ -405,7 +449,7 @@
 
         if k == 0:
             tail_t[tail : 2 * tail, :] = prod_t[0, main:width, :]
-        root_moves[k][2].wait_recv()
+        arrived(root_moves[k])
 
         def squares(part):
             return jnp.sum(part * part, axis=0, keepdims=True)
@@ -436,9 +480,17 @@
             back_copy(k, d).start()
             return total
 
+        def hold(d, total):
+            s = peer(d)
+            return pieces(s, put_in(backs[k], s), total)
+
         lanes = main if k == 0 else wide
         none = (jnp.zeros((1, lanes), jnp.float32), jnp.zeros((1, 128), jnp.float32))
-        total = lax.fori_loop(1, shards, one, none)
+        if k == 0:
+            total = lax.fori_loop(1, EARLY, one, none)
+            total = lax.fori_loop(EARLY, shards, hold, total)
+        else:
+            total = lax.fori_loop(1, shards, one, none)
         total = pieces(me, put_in(ins[k], me), total)
         sums[t, 1, k] = jnp.full((8, 128), jnp.sum(total[0]), jnp.float32)
         if k == 1:
@@ -483,8 +535,11 @@
     outs = []
     for k in range(slots):
         pass_on(grad_moves[k])
-        for hop in (0, 2):
-            grad_moves[k][hop].wait_recv()
+        if k == 1:
+            for d in range(EARLY, shards):
+                back_copy(0, d).start()
+        grad_moves[k][0].wait_recv()
+        arrived(grad_moves[k])
         precondition(k)
         if k + 1 < slots:
             moments(k + 1)
@@ -566,19 +621,28 @@
             back_copy(k, d).wait_send()
 
     for k in range(slots):
-        for move in root_moves[k] + grad_moves[k]:
-            move.wait_send()
+        for moves in (root_moves[k], grad_moves[k]):
+            for move in [moves[0]] + moves[1] + moves[2]:
+                move.wait_send()
     for move in sum_moves:
         move.wait_send()
     for copy in outs:
         copy.wait()
 
 
-def finish_kernel(weights, update, left, right, moment, weights_out, left_out, right_out, moment_out):
+def finish_kernel(
+    weights, update, left, right, moment, weights_out, left_out, right_out, moment_out, sem
+):
+    copies = [
+        pltpu.make_async_copy(src.at[k], dst.at[k], sem.at[i, k])
+        for i, (src, dst) in enumerate(((left, left_out), (right, right_out), (moment, moment_out)))
+        for k in range(src.shape[0])
+    ]
+    for copy in copies:
+        copy.start()
     weights_out[...] = weights[...] + update[...]
-    left_out[...] = left[...]
-    right_out[...] = right[...]
-    moment_out[...] = moment[...]
+    for copy in copies:
+        copy.wait()
 
 
 def kernel_body(
@@ -628,10 +692,10 @@
             pltpu.VMEM((slots * shards, 8, 128), f32),
             dma(slots, shards),
             dma(slots, shards),
-            dma(slots, 3),
-            dma(slots, 3),
-            dma(slots, 3),
-            dma(slots, 3),
+            dma(slots, 1 + 2 * PIECES),
+            dma(slots, 1 + 2 * PIECES),
+            dma(slots, 1 + 2 * PIECES),
+            dma(slots, 1 + 2 * PIECES),
             dma(slots, shards),
             dma(slots, shards),
             dma(3),
@@ -653,15 +717,12 @@
         right_gram_stats,
         flip(adam_second_moment),
     )
-    part = slots * width // blocks
-    strip = pl.BlockSpec((1, rows, width), lambda i: (i, 0, 0))
-    band = pl.BlockSpec((1, part, side), lambda i: (i * part // width, i % (width // part), 0))
     new_weights, new_left, new_right, new_moment = pl.pallas_call(
         finish_kernel,
-        grid=(blocks,),
         out_shape=(jax.ShapeDtypeStruct((blocks, rows, width), f32), stat, stat, stat),
-        in_specs=[strip, strip, band, band, band],
-        out_specs=(strip, band, band, band),
+        in_specs=[vmem, vmem, hbm, hbm, hbm],
+        out_specs=(vmem, hbm, hbm, hbm),
+        scratch_shapes=[dma(3, slots)],
         compiler_params=pltpu.CompilerParams(vmem_limit_bytes=56 * 2**20),
     )(weights, update, new_left, new_right, new_moment)
     return (new_weights, new_left, new_right, flip(new_moment))
@@ -678,6 +739,9 @@
         and slots == 2
         and rows % 16 == 0
         and width % 96 == 0
+        and width // PIECES % 32 == 0
+        and slots * PIECES < shards <= EARLY + PIECES
+        and EARLY < shards
         and width <= TILE - 96
         and 0 < width % 128 <= 64
         and side % TILE == 0

time: 102 us -> 338 us (3.31)
  the two profiles are of different devices: /device:TPU:25 before, /device:TPU:0 now
where the time goes in v3:
time: 338 us
  Pallas kernels  335 us (99%)
    pallas_call x1, Pallas kernels, kernel_body(): pl.pallas_call(finish_kernel, out_shape=(jax.ShapeDtypeStruct((blocks, ro...  246 us
    pallas_call x1, Pallas kernels, kernel_body(): pl.pallas_call(functools.partial(step_kernel, shards), out_shape=(jax.Sha...  89.5 us

profile of v3, /device:TPU:0, one launch (start us, length us, event | category | flops | bytes accessed | tf_op | source)
XLA Modules:
  0.0 337.5 jit_solution(1385392570943778588)
XLA Ops:
  0.6 0.0 copy-start
  0.6 1.2 copy-done
  1.8 0.0 copy-start.1
  1.8 0.7 copy-done.1
  2.5 89.5 %shard_map.111 = (f32[8,144,288]{2,1,0:T(8,128)}, f32[2,288,1152]{2,1,0:T(8,128)}, f32[2,288,1152]{2,1,0:T(8,128)}, f32[2,288,1152]{2,1,0:T(8,128)}) custom-call(s32[8]{0:T(128)S(1)} %copy-done.1, bf16[8,144,288]{2,1,0:T(8,128)(2,1)S(1)} %copy-done, bf16[2,288,1152]{2,1,0:T(8,128)(2,1)} %bitcast.5, bf16[2,288,1152]{2,1,0:T(8,128)(2,1)} %bitcast.6, ...), custom_call_target="tpu_custom_call" | custom-call | tf_op jit(solution)/shard_map/pallas_call | solution.py:670
  91.9 245.6 %shard_map.112 = (f32[8,144,288]{2,1,0:T(8,128)}, f32[2,288,1152]{2,1,0:T(8,128)}, f32[2,288,1152]{2,1,0:T(8,128)}, f32[2,288,1152]{2,1,0:T(8,128)}) custom-call(f32[8,144,288]{2,1,0:T(8,128)} %weights.1, f32[8,144,288]{2,1,0:T(8,128)} %get-tuple-element.12.update, f32[2,288,1152]{2,1,0:T(8,128)} %get-tuple-element.13.left, ...), custom_call_target="tpu_custom_call" | custom-call | tf_op jit(solution)/shard_map/pallas_call | solution.py:720
Async XLA Ops:
  0.6 1.2 copy-start
  1.8 0.7 copy-start.1

commit v4 on v2

--- a/solution.py
+++ b/solution.py
@@ -116,17 +116,19 @@
 
 def step_kernel(
     shards,
-    owner_ref,
-    grad_ref,
-    right_root_ref,
+    owner_hbm,
+    grad_hbm,
+    right_root_hbm,
     left_root_hbm,
     left_hbm,
     right_hbm,
     moment_hbm,
-    update_ref,
-    new_left_hbm,
-    new_right_hbm,
-    new_moment_hbm,
+    in_0,
+    in_1,
+    ratios,
+    left,
+    right,
+    moment,
     out_0,
     out_1,
     own_0,
@@ -137,13 +139,10 @@
     tail_t,
     back_0,
     back_1,
-    in_0,
-    in_1,
-    left,
-    right,
-    moment,
     sums,
-    ratios,
+    owner_ref,
+    grad_ref,
+    right_root_ref,
     s1_send,
     s1_recv,
     g_send,
@@ -157,7 +156,7 @@
     rat_send,
     rat_recv,
     in_sem,
-    out_sem,
+    own_sem,
 ):
     me = lax.axis_index("shard")
     t = lax.axis_index("tensor")
@@ -196,7 +195,13 @@
             ((moment_hbm, moment), (left_hbm, left), (right_hbm, right))
         )
     ]
-    for copy in root_in:
+    first_in = [
+        pltpu.make_async_copy(src, dst, in_sem.at[slots + 3 + i])
+        for i, (src, dst) in enumerate(
+            ((owner_hbm, owner_ref), (grad_hbm, grad_ref), (right_root_hbm, right_root_ref))
+        )
+    ]
+    for copy in first_in + root_in:
         copy.start()
 
     barrier = pltpu.get_barrier_semaphore()
@@ -207,6 +212,8 @@
 
     for other in (sib, across, diag):
         pl.semaphore_signal(barrier, inc=1, device_id=(me, other), device_id_type=MESH)
+
+    first_in[0].wait()
 
     owners = [owner_ref[b] for b in range(blocks)]
     slot_of = []
@@ -238,6 +245,7 @@
         )
         return first[:, :main], ends.astype(jnp.bfloat16), second[:, :main]
 
+    first_in[1].wait()
     pl.semaphore_wait(barrier, shards - 1 + 3)
 
     def s1_copy(k, d):
@@ -373,8 +381,7 @@
         total = lax.fori_loop(0, width // chunk, one, jnp.zeros((1, side), jnp.float32))
         sums[t, 0, k] = jnp.full((8, 128), jnp.sum(total), jnp.float32)
 
-    def back_copy(k, d):
-        s = peer(d)
+    def back_copy(k, s):
         return pltpu.make_async_remote_copy(
             src_ref=backs[k].at[s],
             dst_ref=ins[k].at[me],
@@ -383,6 +390,10 @@
             device_id=(s, t),
             device_id_type=MESH,
         )
+
+    own_copies = [
+        pltpu.make_async_copy(backs[k].at[me], ins[k].at[me], own_sem.at[k]) for k in range(slots)
+    ]
 
     def back_arrival(k, d):
         s = peer(d)
@@ -407,39 +418,33 @@
             tail_t[tail : 2 * tail, :] = prod_t[0, main:width, :]
         root_moves[k][2].wait_recv()
 
-        def squares(part):
-            return jnp.sum(part * part, axis=0, keepdims=True)
-
-        def pieces(s, put, total):
-            if k == 0:
-                part = mm(left_root[0, strip(s), :], prod_t[0, 0:main, :], NT)
-                put(part)
-                return total[0] + squares(part), total[1]
-            part = mm(left_root[1, strip(s), :], prod_t[1], NT)
-            ends = mm(left_root[0, strip(s), :], tail_t[...], NT)
-            put(part, ends)
-            return total[0] + squares(part), total[1] + squares(ends)
-
-        def put_in(ref, s):
-            def put(part, ends=None):
-                if ends is None:
-                    ref[s] = part.astype(jnp.bfloat16)
+        group = shards // 2
+        lanes = main if k == 0 else wide
+        squares, end_squares = jnp.zeros((1, lanes), jnp.float32), jnp.zeros((1, 128), jnp.float32)
+        for turn in range(2):
+            first = lax.rem(me // group + 1 + turn, 2) * group
+            band = pl.ds(pl.multiple_of(first * rows, 32), group * rows)
+            part = mm(left_root[k, band, :], prod_t[k, 0:lanes, :], NT)
+            squares += jnp.sum(part * part, axis=0, keepdims=True)
+            if k == 1:
+                ends = mm(left_root[0, band, :], tail_t[...], NT)
+                end_squares += jnp.sum(ends * ends, axis=0, keepdims=True)
+            for j in range(group):
+                piece = part[j * rows : (j + 1) * rows]
+                if k == 0:
+                    back_0[first + j] = piece.astype(jnp.bfloat16)
                 else:
-                    ref[s, :, 0:main] = part[:, 0:main].astype(jnp.bfloat16)
-                    ref[s, :, main:wide] = (part[:, main:wide] + ends).astype(jnp.bfloat16)
-
-            return put
-
-        def one(d, total):
-            s = peer(d)
-            total = pieces(s, put_in(backs[k], s), total)
-            back_copy(k, d).start()
-            return total
-
-        lanes = main if k == 0 else wide
-        none = (jnp.zeros((1, lanes), jnp.float32), jnp.zeros((1, 128), jnp.float32))
-        total = lax.fori_loop(1, shards, one, none)
-        total = pieces(me, put_in(ins[k], me), total)
+                    back_1[first + j, :, 0:main] = piece[:, 0:main].astype(jnp.bfloat16)
+                    back_1[first + j, :, main:wide] = (
+                        piece[:, main:wide] + ends[j * rows : (j + 1) * rows]
+                    ).astype(jnp.bfloat16)
+            for j in range(group):
+                s = first + lax.rem(lax.rem(me, group) + 1 + j, group)
+                if turn == 1 and j == group - 1:
+                    own_copies[k].start()
+                else:
+                    back_copy(k, s).start()
+        total = (squares, end_squares)
         sums[t, 1, k] = jnp.full((8, 128), jnp.sum(total[0]), jnp.float32)
         if k == 1:
             sums[t, 1, 0] = sums[t, 1, 0] + jnp.full((8, 128), jnp.sum(total[1]), jnp.float32)
@@ -450,7 +455,6 @@
 
     def grams(k):
         rows_t = mm(select, grad_t[k, :, pl.ds(start, TILE)], NT).astype(jnp.bfloat16)
-        out = []
 
         @pl.loop(0, side // TILE)
         def _(j):
@@ -462,16 +466,10 @@
                 grad_t[k, t_rows, :], grad_t[k, at, :], NT
             ) / MODEL_WIDTH
 
-        for i, (src, dst) in enumerate(
-            ((left, new_left_hbm), (right, new_right_hbm), (moment, new_moment_hbm))
-        ):
-            copy = pltpu.make_async_copy(src.at[k], dst.at[k], out_sem.at[k, i])
-            copy.start()
-            out.append(copy)
-        return out
 
     for k in range(slots):
         mirror(k)
+    first_in[2].wait()
     turn_panel(0)
     for k in range(slots):
         pass_on(root_moves[k])
@@ -480,7 +478,6 @@
     moments(0)
     turn_panel(1)
 
-    outs = []
     for k in range(slots):
         pass_on(grad_moves[k])
         for hop in (0, 2):
@@ -488,7 +485,7 @@
         precondition(k)
         if k + 1 < slots:
             moments(k + 1)
-            outs += grams(k)
+            grams(k)
 
     sum_moves = [
         pltpu.make_async_remote_copy(
@@ -503,7 +500,7 @@
     ]
     for move in sum_moves:
         move.start()
-    outs += grams(slots - 1)
+    grams(slots - 1)
     for move in sum_moves:
         move.wait_recv()
 
@@ -546,39 +543,60 @@
         for k in range(slots):
             back_arrival(k, d).wait_recv()
 
-    for b in range(blocks):
-        scale = -learn_rate * ratios[slot_of[b]][0:1, 0:1]
-        first, second = in_0[owners[b]], in_1[owners[b]]
-        at_first = slot_of[b] == owners[b] * slots
-        ends = second[:, main:wide].astype(jnp.float32)
-        update_ref[b, :, 0:main] = scale * jnp.where(at_first, first, second[:, 0:main]).astype(
-            jnp.float32
-        )
-        update_ref[b, :, main:width] = scale * jnp.where(
-            at_first, ends[:, tail : 2 * tail], ends[:, 0:tail]
-        )
-
     @pl.loop(1, shards)
     def _(d):
         ratio_copy(d).wait_send()
         for k in range(slots):
             s1_copy(k, d).wait_send()
-            back_copy(k, d).wait_send()
+            back_copy(k, peer(d)).wait_send()
 
     for k in range(slots):
         for move in root_moves[k] + grad_moves[k]:
             move.wait_send()
     for move in sum_moves:
         move.wait_send()
-    for copy in outs:
+    for copy in own_copies:
         copy.wait()
 
 
-def finish_kernel(weights, update, left, right, moment, weights_out, left_out, right_out, moment_out):
-    weights_out[...] = weights[...] + update[...]
-    left_out[...] = left[...]
-    right_out[...] = right[...]
-    moment_out[...] = moment[...]
+def finish_kernel(
+    owners,
+    weights,
+    first,
+    second,
+    ratios,
+    left,
+    right,
+    moment,
+    weights_out,
+    left_out,
+    right_out,
+    moment_out,
+    sem,
+):
+    copies = [
+        pltpu.make_async_copy(src.at[k], dst.at[k], sem.at[i, k])
+        for i, (src, dst) in enumerate(((left, left_out), (right, right_out), (moment, moment_out)))
+        for k in range(src.shape[0])
+    ]
+    for copy in copies:
+        copy.start()
+    blocks, _, width = weights.shape
+    main = first.shape[2]
+    tail = width - main
+    for b in range(blocks):
+        rank = jnp.int32(0)
+        for c in range(b):
+            rank = rank + jnp.where(owners[c] == owners[b], 1, 0)
+        scale = -learn_rate * ratios[owners[b] * SLOTS + rank][0:1, 0:1]
+        other = second[owners[b]]
+        whole = jnp.where(rank == 0, first[owners[b]], other[:, 0:main]).astype(jnp.float32)
+        ends = other[:, main:].astype(jnp.float32)
+        ends = jnp.where(rank == 0, ends[:, tail : 2 * tail], ends[:, 0:tail])
+        weights_out[b, :, 0:main] = weights[b, :, 0:main] + scale * whole
+        weights_out[b, :, main:] = weights[b, :, main:] + scale * ends
+    for copy in copies:
+        copy.wait()
 
 
 def kernel_body(
@@ -603,11 +621,18 @@
     vmem = pl.BlockSpec(memory_space=pltpu.VMEM)
     dma = lambda *shape: pltpu.SemaphoreType.DMA(shape)
     stat = jax.ShapeDtypeStruct((slots, width, side), f32)
-    update, new_left, new_right, new_moment = pl.pallas_call(
+    first, second, ratios, new_left, new_right, new_moment = pl.pallas_call(
         functools.partial(step_kernel, shards),
-        out_shape=(jax.ShapeDtypeStruct((blocks, rows, width), f32), stat, stat, stat),
-        in_specs=[pl.BlockSpec(memory_space=pltpu.SMEM), vmem, vmem, hbm, hbm, hbm, hbm],
-        out_specs=(vmem, hbm, hbm, hbm),
+        out_shape=(
+            jax.ShapeDtypeStruct((shards, rows, main), bf16),
+            jax.ShapeDtypeStruct((shards, rows, wide), bf16),
+            jax.ShapeDtypeStruct((slots * shards, 8, 128), f32),
+            stat,
+            stat,
+            stat,
+        ),
+        in_specs=[pl.BlockSpec(memory_space=pltpu.HBM)] * 7,
+        out_specs=(hbm, hbm, vmem, vmem, vmem, vmem),
         scratch_shapes=[
             pltpu.VMEM((shards, rows, wide), bf16),
             pltpu.VMEM((shards, rows, main), bf16),
@@ -619,13 +644,10 @@
             pltpu.VMEM((128, side), bf16),
             pltpu.VMEM((shards, rows, main), bf16),
             pltpu.VMEM((shards, rows, wide), bf16),
-            pltpu.VMEM((shards, rows, main), bf16),
-            pltpu.VMEM((shards, rows, wide), bf16),
-            pltpu.VMEM((slots, width, side), f32),
-            pltpu.VMEM((slots, width, side), f32),
-            pltpu.VMEM((slots, width, side), f32),
             pltpu.VMEM((4, 2, slots, 8, 128), f32),
-            pltpu.VMEM((slots * shards, 8, 128), f32),
+            pltpu.SMEM((blocks,), jnp.int32),
+            pltpu.VMEM((blocks, rows, width), bf16),
+            pltpu.VMEM((slots, width, side), bf16),
             dma(slots, shards),
             dma(slots, shards),
             dma(slots, 3),
@@ -638,11 +660,11 @@
             dma(3),
             dma(shards),
             dma(shards),
-            dma(slots + 3),
-            dma(slots, 3),
+            dma(slots + 6),
+            dma(slots),
         ],
         compiler_params=pltpu.CompilerParams(
-            collective_id=0, has_side_effects=True, vmem_limit_bytes=52 * 2**20
+            collective_id=0, has_side_effects=True, vmem_limit_bytes=40 * 2**20
         ),
     )(
         owner_list,
@@ -653,17 +675,14 @@
         right_gram_stats,
         flip(adam_second_moment),
     )
-    part = slots * width // blocks
-    strip = pl.BlockSpec((1, rows, width), lambda i: (i, 0, 0))
-    band = pl.BlockSpec((1, part, side), lambda i: (i * part // width, i % (width // part), 0))
     new_weights, new_left, new_right, new_moment = pl.pallas_call(
         finish_kernel,
-        grid=(blocks,),
+        in_specs=[pl.BlockSpec(memory_space=pltpu.SMEM)] + [vmem] * 7,
+        out_specs=(vmem, hbm, hbm, hbm),
         out_shape=(jax.ShapeDtypeStruct((blocks, rows, width), f32), stat, stat, stat),
-        in_specs=[strip, strip, band, band, band],
-        out_specs=(strip, band, band, band),
-        compiler_params=pltpu.CompilerParams(vmem_limit_bytes=56 * 2**20),
-    )(weights, update, new_left, new_right, new_moment)
+        scratch_shapes=[dma(3, slots)],
+        compiler_params=pltpu.CompilerParams(vmem_limit_bytes=24 * 2**20),
+    )(owner_list, weights, first, second, ratios, new_left, new_right, new_moment)
     return (new_weights, new_left, new_right, flip(new_moment))
 
 
@@ -677,6 +696,8 @@
         tensor == 4
         and slots == 2
         and rows % 16 == 0
+        and shards % 2 == 0
+        and rows * shards // 2 % 32 == 0
         and width % 96 == 0
         and width <= TILE - 96
         and 0 < width % 128 <= 64

time: 102 us -> 96.3 us (0.944)
  the two profiles are of different devices: /device:TPU:25 before, /device:TPU:0 now
where the time goes in v4:
time: 96.3 us; the launch traced here: 96.1 us
  Pallas kernels  91 us (94%)
  local copies, waits for them, and re-layouts  4.46 us (5%)
    pallas_call x1, Pallas kernels, kernel_body(): pl.pallas_call(functools.partial(step_kernel, shards), out_shape=(jax.Sha...  85.6 us
    pallas_call x1, Pallas kernels, kernel_body(): pl.pallas_call(finish_kernel, in_specs=[pl.BlockSpec(memory_space=pltpu.S...  5.38 us
    unnamed x10, local copies, waits for them, and re-layouts  4.46 us

profile of v4, /device:TPU:0, one launch (start us, length us, event | category | flops | bytes accessed | tf_op | source)
XLA Modules:
  0.0 96.1 jit_solution(15297726847781829468)
XLA Ops:
  0.6 0.0 copy-start.1
  0.6 1.3 %copy-done.1 = bf16[2,1152,288]{1,2,0:T(8,128)(2,1)S(1)} copy-done((bf16[2,1152,288]{1,2,0:T(8,128)(2,1)S(1)}, bf16[2,1152,288]{1,2,0:T(8,128)(2,1)}, u32[]{:S(2)}) %copy-start.1) | copy-done | bytes 1327128
  2.0 0.0 copy-start.2
  2.0 1.3 %copy-done.2 = bf16[2,1152,288]{1,2,0:T(8,128)(2,1)S(1)} copy-done((bf16[2,1152,288]{1,2,0:T(8,128)(2,1)S(1)}, bf16[2,1152,288]{1,2,0:T(8,128)(2,1)}, u32[]{:S(2)}) %copy-start.2) | copy-done | bytes 1327128
  3.3 0.0 copy-start.3
  3.3 1.2 %copy-done.3 = bf16[8,144,288]{2,1,0:T(8,128)(2,1)S(1)} copy-done((bf16[8,144,288]{2,1,0:T(8,128)(2,1)S(1)}, bf16[8,144,288]{2,1,0:T(8,128)(2,1)}, u32[]{:S(2)}) %copy-start.3) | copy-done | bytes 663576
  4.4 0.0 copy-start.4
  4.4 0.7 copy-done.4
  5.1 0.0 copy-start
  5.1 85.6 %shard_map.111 = (bf16[8,144,256]{2,1,0:T(8,128)(2,1)S(1)}, bf16[8,144,384]{2,1,0:T(8,128)(2,1)S(1)}, f32[16,8,128]{2,1,0:T(8,128)S(1)}, f32[2,288,1152]{2,1,0:T...) custom-call(s32[8]{0:T(128)S(1)} %copy-done.4, bf16[8,144,288]{2,1,0:T(8,128)(2,1)S(1)} %copy-done.3, ...), custom_call_target="tpu_custom_call" | custom-call | tf_op jit(solution)/shard_map/pallas_call | solution.py:624
  90.7 0.0 copy-done
  90.7 5.4 %shard_map.112 = (f32[8,144,288]{2,1,0:T(8,128)}, f32[2,288,1152]{2,1,0:T(8,128)}, f32[2,288,1152]{2,1,0:T(8,128)}, f32[2,288,1152]{2,1,0:T(8,128)}) custom-call(s32[8]{0:T(128)S(1)} %copy-done.4, f32[8,144,288]{2,1,0:T(8,128)S(1)} %copy-done, bf16[8,144,256]{2,1,0:T(8,128)(2,1)S(1)} %get-tuple-element.14.first, ...), custom_call_target="tpu_custom_call" | custom-call | tf_op jit(solution)/shard_map/pallas_call | solution.py:678
Async XLA Ops:
  0.6 1.3 %copy-start.1 = (bf16[2,1152,288]{1,2,0:T(8,128)(2,1)S(1)}, bf16[2,1152,288]{1,2,0:T(8,128)(2,1)}, u32[]{:S(2)}) copy-start(bf16[2,1152,288]{1,2,0:T(8,128)(2,1)} %param.14) | copy-start | bytes 3981316
  2.0 1.3 %copy-start.2 = (bf16[2,1152,288]{1,2,0:T(8,128)(2,1)S(1)}, bf16[2,1152,288]{1,2,0:T(8,128)(2,1)}, u32[]{:S(2)}) copy-start(bf16[2,1152,288]{1,2,0:T(8,128)(2,1)} %param.13) | copy-start | bytes 3981316
  3.3 1.2 %copy-start.3 = (bf16[8,144,288]{2,1,0:T(8,128)(2,1)S(1)}, bf16[8,144,288]{2,1,0:T(8,128)(2,1)}, u32[]{:S(2)}) copy-start(bf16[8,144,288]{2,1,0:T(8,128)(2,1)} %grad_hbm.1) | copy-start | bytes 1990660
  4.4 0.7 copy-start.4
  5.1 85.6 %copy-start = (f32[8,144,288]{2,1,0:T(8,128)S(1)}, f32[8,144,288]{2,1,0:T(8,128)}, u32[]{:S(2)}) copy-start(f32[8,144,288]{2,1,0:T(8,128)} %weights.1) | copy-start | bytes 3981316

commit v5 on v4

--- a/solution.py
+++ b/solution.py
@@ -177,8 +177,11 @@
     t_rows = pl.ds(pl.multiple_of(t * width, 32), width)
     across_rows = pl.ds(pl.multiple_of(across * width, 32), width)
 
+    group = shards // 2
+
     def peer(d):
-        return lax.rem(me + d, shards)
+        far = jnp.where(d <= group, 1, 0)
+        return lax.rem(me // group + far, 2) * group + lax.rem(me + d, group)
 
     def strip(s):
         return pl.ds(pl.multiple_of(s * rows, 16), rows)
@@ -418,7 +421,6 @@
             tail_t[tail : 2 * tail, :] = prod_t[0, main:width, :]
         root_moves[k][2].wait_recv()
 
-        group = shards // 2
         lanes = main if k == 0 else wide
         squares, end_squares = jnp.zeros((1, lanes), jnp.float32), jnp.zeros((1, 128), jnp.float32)
         for turn in range(2):

time: 96.3 us -> 101 us (1.049)
  Pallas kernels: 91 us -> 95.4 us
    pallas_call x1, Pallas kernels: 85.6 us -> 90.1 us  [kernel_body(): pl.pallas_call(functools.partial(step_kernel, shards), out_shape=(jax.Sha...]
where the time goes in v5:
time: 101 us
  Pallas kernels  95.4 us (94%)
  local copies, waits for them, and re-layouts  4.46 us (4%)
    pallas_call x1, Pallas kernels, kernel_body(): pl.pallas_call(functools.partial(step_kernel, shards), out_shape=(jax.Sha...  90.1 us
    pallas_call x1, Pallas kernels, kernel_body(): pl.pallas_call(finish_kernel, in_specs=[pl.BlockSpec(memory_space=pltpu.S...  5.38 us
    unnamed x10, local copies, waits for them, and re-layouts  4.46 us

profile of v5, /device:TPU:0, one launch (start us, length us, event | category | flops | bytes accessed | tf_op | source)
XLA Modules:
  0.0 100.6 jit_solution(16547413283377714316)
XLA Ops:
  0.6 0.0 copy-start.1
  0.6 1.3 %copy-done.1 = bf16[2,1152,288]{1,2,0:T(8,128)(2,1)S(1)} copy-done((bf16[2,1152,288]{1,2,0:T(8,128)(2,1)S(1)}, bf16[2,1152,288]{1,2,0:T(8,128)(2,1)}, u32[]{:S(2)}) %copy-start.1) | copy-done | bytes 1327128
  2.0 0.0 copy-start.2
  2.0 1.3 %copy-done.2 = bf16[2,1152,288]{1,2,0:T(8,128)(2,1)S(1)} copy-done((bf16[2,1152,288]{1,2,0:T(8,128)(2,1)S(1)}, bf16[2,1152,288]{1,2,0:T(8,128)(2,1)}, u32[]{:S(2)}) %copy-start.2) | copy-done | bytes 1327128
  3.3 0.0 copy-start.3
  3.3 1.2 %copy-done.3 = bf16[8,144,288]{2,1,0:T(8,128)(2,1)S(1)} copy-done((bf16[8,144,288]{2,1,0:T(8,128)(2,1)S(1)}, bf16[8,144,288]{2,1,0:T(8,128)(2,1)}, u32[]{:S(2)}) %copy-start.3) | copy-done | bytes 663576
  4.4 0.0 copy-start.4
  4.4 0.7 copy-done.4
  5.1 0.0 copy-start
  5.1 90.1 %shard_map.111 = (bf16[8,144,256]{2,1,0:T(8,128)(2,1)S(1)}, bf16[8,144,384]{2,1,0:T(8,128)(2,1)S(1)}, f32[16,8,128]{2,1,0:T(8,128)S(1)}, f32[2,288,1152]{2,1,0:T...) custom-call(s32[8]{0:T(128)S(1)} %copy-done.4, bf16[8,144,288]{2,1,0:T(8,128)(2,1)S(1)} %copy-done.3, ...), custom_call_target="tpu_custom_call" | custom-call | tf_op jit(solution)/shard_map/pallas_call | solution.py:626
  95.2 0.0 copy-done
  95.2 5.4 %shard_map.112 = (f32[8,144,288]{2,1,0:T(8,128)}, f32[2,288,1152]{2,1,0:T(8,128)}, f32[2,288,1152]{2,1,0:T(8,128)}, f32[2,288,1152]{2,1,0:T(8,128)}) custom-call(s32[8]{0:T(128)S(1)} %copy-done.4, f32[8,144,288]{2,1,0:T(8,128)S(1)} %copy-done, bf16[8,144,256]{2,1,0:T(8,128)(2,1)S(1)} %get-tuple-element.14.first, ...), custom_call_target="tpu_custom_call" | custom-call | tf_op jit(solution)/shard_map/pallas_call | solution.py:680
Async XLA Ops:
  0.6 1.3 %copy-start.1 = (bf16[2,1152,288]{1,2,0:T(8,128)(2,1)S(1)}, bf16[2,1152,288]{1,2,0:T(8,128)(2,1)}, u32[]{:S(2)}) copy-start(bf16[2,1152,288]{1,2,0:T(8,128)(2,1)} %param.14) | copy-start | bytes 3981316
  2.0 1.3 %copy-start.2 = (bf16[2,1152,288]{1,2,0:T(8,128)(2,1)S(1)}, bf16[2,1152,288]{1,2,0:T(8,128)(2,1)}, u32[]{:S(2)}) copy-start(bf16[2,1152,288]{1,2,0:T(8,128)(2,1)} %param.13) | copy-start | bytes 3981316
  3.3 1.2 %copy-start.3 = (bf16[8,144,288]{2,1,0:T(8,128)(2,1)S(1)}, bf16[8,144,288]{2,1,0:T(8,128)(2,1)}, u32[]{:S(2)}) copy-start(bf16[8,144,288]{2,1,0:T(8,128)(2,1)} %grad_hbm.1) | copy-start | bytes 1990660
  4.4 0.7 copy-start.4
  5.1 90.1 %copy-start = (f32[8,144,288]{2,1,0:T(8,128)S(1)}, f32[8,144,288]{2,1,0:T(8,128)}, u32[]{:S(2)}) copy-start(f32[8,144,288]{2,1,0:T(8,128)} %weights.1) | copy-start | bytes 3981316

commit v6 on v4

--- a/solution.py
+++ b/solution.py
@@ -438,12 +438,11 @@
                     back_1[first + j, :, main:wide] = (
                         piece[:, main:wide] + ends[j * rows : (j + 1) * rows]
                     ).astype(jnp.bfloat16)
-            for j in range(group):
-                s = first + lax.rem(lax.rem(me, group) + 1 + j, group)
-                if turn == 1 and j == group - 1:
-                    own_copies[k].start()
-                else:
-                    back_copy(k, s).start()
+        @pl.loop(1, shards)
+        def _(d):
+            back_copy(k, peer(d)).start()
+
+        own_copies[k].start()
         total = (squares, end_squares)
         sums[t, 1, k] = jnp.full((8, 128), jnp.sum(total[0]), jnp.float32)
         if k == 1:

time: 96.3 us -> 99.2 us (1.030)
  the two profiles are of different devices: /device:TPU:0 before, /device:TPU:25 now
where the time goes in v6:
time: 99.2 us; the launch traced here: 99 us
  Pallas kernels  93.8 us (95%)
  local copies, waits for them, and re-layouts  4.46 us (4%)
    pallas_call x1, Pallas kernels, kernel_body(): pl.pallas_call(functools.partial(step_kernel, shards), out_shape=(jax.Sha...  88.5 us
    pallas_call x1, Pallas kernels, kernel_body(): pl.pallas_call(finish_kernel, in_specs=[pl.BlockSpec(memory_space=pltpu.S...  5.37 us
    unnamed x10, local copies, waits for them, and re-layouts  4.46 us

profile of v6, /device:TPU:25, one launch (start us, length us, event | category | flops | bytes accessed | tf_op | source)
XLA Modules:
  0.0 99.0 jit_solution(5312323385226197372)
XLA Ops:
  0.6 0.0 copy-start.1
  0.6 1.3 %copy-done.1 = bf16[2,1152,288]{1,2,0:T(8,128)(2,1)S(1)} copy-done((bf16[2,1152,288]{1,2,0:T(8,128)(2,1)S(1)}, bf16[2,1152,288]{1,2,0:T(8,128)(2,1)}, u32[]{:S(2)}) %copy-start.1) | copy-done | bytes 1327128
  2.0 0.0 copy-start.2
  2.0 1.3 %copy-done.2 = bf16[2,1152,288]{1,2,0:T(8,128)(2,1)S(1)} copy-done((bf16[2,1152,288]{1,2,0:T(8,128)(2,1)S(1)}, bf16[2,1152,288]{1,2,0:T(8,128)(2,1)}, u32[]{:S(2)}) %copy-start.2) | copy-done | bytes 1327128
  3.3 0.0 copy-start.3
  3.3 1.2 %copy-done.3 = bf16[8,144,288]{2,1,0:T(8,128)(2,1)S(1)} copy-done((bf16[8,144,288]{2,1,0:T(8,128)(2,1)S(1)}, bf16[8,144,288]{2,1,0:T(8,128)(2,1)}, u32[]{:S(2)}) %copy-start.3) | copy-done | bytes 663576
  4.4 0.0 copy-start.4
  4.4 0.7 copy-done.4
  5.1 0.0 copy-start
  5.1 88.5 %shard_map.111 = (bf16[8,144,256]{2,1,0:T(8,128)(2,1)S(1)}, bf16[8,144,384]{2,1,0:T(8,128)(2,1)S(1)}, f32[16,8,128]{2,1,0:T(8,128)S(1)}, f32[2,288,1152]{2,1,0:T...) custom-call(s32[8]{0:T(128)S(1)} %copy-done.4, bf16[8,144,288]{2,1,0:T(8,128)(2,1)S(1)} %copy-done.3, ...), custom_call_target="tpu_custom_call" | custom-call | tf_op jit(solution)/shard_map/pallas_call | solution.py:623
  93.6 0.0 copy-done
  93.6 5.4 %shard_map.112 = (f32[8,144,288]{2,1,0:T(8,128)}, f32[2,288,1152]{2,1,0:T(8,128)}, f32[2,288,1152]{2,1,0:T(8,128)}, f32[2,288,1152]{2,1,0:T(8,128)}) custom-call(s32[8]{0:T(128)S(1)} %copy-done.4, f32[8,144,288]{2,1,0:T(8,128)S(1)} %copy-done, bf16[8,144,256]{2,1,0:T(8,128)(2,1)S(1)} %get-tuple-element.14.first, ...), custom_call_target="tpu_custom_call" | custom-call | tf_op jit(solution)/shard_map/pallas_call | solution.py:677
Async XLA Ops:
  0.6 1.3 %copy-start.1 = (bf16[2,1152,288]{1,2,0:T(8,128)(2,1)S(1)}, bf16[2,1152,288]{1,2,0:T(8,128)(2,1)}, u32[]{:S(2)}) copy-start(bf16[2,1152,288]{1,2,0:T(8,128)(2,1)} %param.14) | copy-start | bytes 3981316
  2.0 1.3 %copy-start.2 = (bf16[2,1152,288]{1,2,0:T(8,128)(2,1)S(1)}, bf16[2,1152,288]{1,2,0:T(8,128)(2,1)}, u32[]{:S(2)}) copy-start(bf16[2,1152,288]{1,2,0:T(8,128)(2,1)} %param.13) | copy-start | bytes 3981316
  3.3 1.2 %copy-start.3 = (bf16[8,144,288]{2,1,0:T(8,128)(2,1)S(1)}, bf16[8,144,288]{2,1,0:T(8,128)(2,1)}, u32[]{:S(2)}) copy-start(bf16[8,144,288]{2,1,0:T(8,128)(2,1)} %grad_hbm.1) | copy-start | bytes 1990660
  4.4 0.7 copy-start.4
  5.1 88.5 %copy-start = (f32[8,144,288]{2,1,0:T(8,128)S(1)}, f32[8,144,288]{2,1,0:T(8,128)}, u32[]{:S(2)}) copy-start(f32[8,144,288]{2,1,0:T(8,128)} %weights.1) | copy-start | bytes 3981316
